TPU v7x, 32 devices: a whole 2x2x4 slice. The times are simulated.
32 devices in a mesh: groups: 2 (over y), expert: 4 (over z), sub: 2 (over x), pair: 2 (over core).
Axes of the slice: x: 2, y: 2, z: 4, core: 2. Of those that a mesh axis runs over, the one named last changes fastest.
Arguments:
- tokens: bfloat16 [4096, 2048], P(('groups', 'expert', 'sub', 'pair')), parts along dimension 0, may hold values from -6 to 6
- out_grad: bfloat16 [4096, 2048], P(('groups', 'expert', 'sub', 'pair')), parts along dimension 0, may hold values from -6 to 6
- routes: int32 [4096, 8], P(('groups', 'expert', 'sub', 'pair')), parts along dimension 0, may hold values from 0 to 127, as said below
- route_weight: bfloat16 [4096, 8], P(('groups', 'expert', 'sub', 'pair')), parts along dimension 0, may hold values from 0.099609375 to 1
- example_id: int32 [4096], P(('groups', 'expert', 'sub', 'pair')), parts along dimension 0, may hold values from 0 to 15, never falling along the last dimension, each value on 1 to 512 neighbouring positions
- gate_w: bfloat16 [4, 2048, 1024], P('expert', 'sub', 'pair'), may hold values from -0.125 to 0.125
- up_w: bfloat16 [4, 2048, 1024], P('expert', 'sub', 'pair'), may hold values from -0.125 to 0.125
- down_w: bfloat16 [4, 1024, 2048], P('expert', 'pair', 'sub'), may hold values from -0.1875 to 0.1875
- proj_grad: bfloat16 [64, 2048], replicated, may hold values from -0.125 to 0.125
- proj_hidden: bfloat16 [64, 1024], P(None, 'pair'), may hold values from -0.1875 to 0.1875
Outputs:
- input_grad: bfloat16 [4096, 2048], P(('groups', 'expert', 'sub', 'pair')), parts along dimension 0
- example_grads: float32 [32, 4, 64, 64], P(('groups', 'expert'), None, ('sub', 'pair')), parts along dimension 0
There are 2 independent parts, one for each index of `groups`. A program takes and returns all parts, laid end to end along the dimension named above; an argument that names none is the same for every part. Nothing has to cross between parts.
Inputs may be any that keep to these rules, and one draw needn't show every extreme that they name: `routes`: each row names 8 different experts. Within the rows of one device (aligned blocks of 128 rows) no expert below 4 is named by more than 10 rows, and one such expert is named by exactly 10 rows in every block.
All inputs are finite; a program needn't handle non-finite values.
Results may differ from a plain program's by a relative error of at most 0.01.
Values may be sent and summed in bfloat16 or wider, within the bound.
A program may use at most 128 MiB of HBM per device.

v0:
```python
import jax
import jax.numpy as jnp
from jax import lax
from jax.sharding import PartitionSpec as P

CAP = 10


def per_device(
    tokens, out_grad, routes, route_weight, example_id, gate_w, up_w, down_w, proj_grad, proj_hidden
):
    owners = lax.axis_size("expert")
    subs = lax.axis_size("sub")
    halves = lax.axis_size("pair")
    half_index = lax.axis_index("pair")
    local_tokens, width = tokens.shape
    fanout = routes.shape[1]
    rank_size = proj_grad.shape[0]
    capacity = CAP
    slots = owners * capacity
    route_flat = routes.reshape(-1)
    inside = route_flat < owners
    owner_hot = (
        (route_flat[:, None] == jnp.arange(owners, dtype=jnp.int32)[None, :]) & inside[:, None]
    ).astype(jnp.int32)
    earlier = jnp.cumsum(owner_hot, axis=0) - owner_hot
    position = jnp.sum(earlier * owner_hot, axis=1)
    target = route_flat * capacity + position
    select = (
        (target[None, :] == jnp.arange(slots, dtype=jnp.int32)[:, None]) & inside[None, :]
    ).astype(jnp.bfloat16)
    pick_token = jnp.sum(select.reshape(slots, local_tokens, fanout), axis=2)
    rows_in = jnp.dot(pick_token, tokens, preferred_element_type=jnp.float32).astype(jnp.bfloat16)
    rows_out = jnp.dot(pick_token, out_grad, preferred_element_type=jnp.float32).astype(
        jnp.bfloat16
    )
    slot_weight = jnp.dot(select, route_weight.reshape(-1), preferred_element_type=jnp.float32)
    rows_grad = (slot_weight[:, None] * rows_out.astype(jnp.float32)).astype(jnp.bfloat16)
    codes = jnp.repeat(example_id + 1, fanout).astype(jnp.bfloat16)
    slot_code = jnp.dot(select, codes, preferred_element_type=jnp.float32).astype(jnp.bfloat16)
    slot_proj = lax.dot_general(
        rows_grad, proj_grad, (((1,), (1,)), ((), ())), preferred_element_type=jnp.float32
    ).astype(jnp.bfloat16)
    rows_in = rows_in.reshape(owners, capacity, width)
    rows_grad = rows_grad.reshape(owners, capacity, width)
    slot_code = slot_code.reshape(owners, capacity)
    slot_proj = slot_proj.reshape(owners, capacity, rank_size)
    grouped = (
        lax.all_gather(rows_in[None], "pair", axis=0, tiled=True),
        lax.all_gather(rows_grad[None], "pair", axis=0, tiled=True),
        lax.all_gather(slot_code[None], "pair", axis=0, tiled=True),
        lax.all_gather(slot_proj[None], "pair", axis=0, tiled=True),
    )
    shared = (
        lax.all_to_all(grouped[0], "expert", split_axis=1, concat_axis=1, tiled=True),
        lax.all_to_all(grouped[1], "expert", split_axis=1, concat_axis=1, tiled=True),
        lax.all_to_all(grouped[2], "expert", split_axis=1, concat_axis=1, tiled=True),
        lax.all_to_all(grouped[3], "expert", split_axis=1, concat_axis=1, tiled=True),
    )
    weights = (
        lax.all_gather(gate_w[0], "sub", axis=0, tiled=True),
        lax.all_gather(up_w[0], "sub", axis=0, tiled=True),
        lax.all_gather(down_w[0], "sub", axis=1, tiled=True),
    )
    gate_local = weights[0]
    up_local = weights[1]
    down_local = weights[2]
    rows_x = shared[0].reshape(-1, width)
    rows_dz = shared[1].reshape(-1, width)
    rows_code = shared[2].reshape(-1)
    rows_proj = shared[3].reshape(-1, rank_size)
    total_rows = rows_x.shape[0]
    gate_pre = jnp.dot(rows_x, gate_local, preferred_element_type=jnp.float32)
    up_pre = jnp.dot(rows_x, up_local, preferred_element_type=jnp.float32)
    sigmoid_gate = jax.nn.sigmoid(gate_pre)
    silu_gate = gate_pre * sigmoid_gate
    hidden = (silu_gate * up_pre).astype(jnp.bfloat16)
    hidden_grad = lax.dot_general(
        rows_dz, down_local, (((1,), (1,)), ((), ())), preferred_element_type=jnp.float32
    )
    gate_grad = (
        hidden_grad * up_pre * sigmoid_gate * (1.0 + gate_pre * (1.0 - sigmoid_gate))
    ).astype(jnp.bfloat16)
    up_grad = (hidden_grad * silu_gate).astype(jnp.bfloat16)
    first = lax.dot_general(
        gate_grad, gate_local, (((1,), (1,)), ((), ())), preferred_element_type=jnp.float32
    )
    second = lax.dot_general(
        up_grad, up_local, (((1,), (1,)), ((), ())), preferred_element_type=jnp.float32
    )
    summed = lax.psum_scatter(
        (first + second).astype(jnp.bfloat16), "pair", scatter_dimension=0, tiled=True
    ).astype(jnp.float32)
    summed = summed.astype(jnp.bfloat16).reshape(owners, capacity, width)
    returned = lax.all_to_all(summed, "expert", split_axis=0, concat_axis=0, tiled=True).reshape(
        slots, width
    )
    input_grad = lax.dot_general(
        pick_token, returned, (((0,), (0,)), ((), ())), preferred_element_type=jnp.float32
    ).astype(jnp.bfloat16)
    hidden_part = lax.dot_general(
        hidden, proj_hidden, (((1,), (1,)), ((), ())), preferred_element_type=jnp.float32
    )
    hidden_full = lax.psum(hidden_part.astype(jnp.bfloat16), "pair").astype(jnp.float32)
    slice_rank = rank_size // (subs * halves)
    proj_split = rows_proj.reshape(total_rows, subs, halves, slice_rank)
    proj_mine = (
        lax.dynamic_slice_in_dim(proj_split, half_index, 1, 2)
        .reshape(total_rows, subs * slice_rank)
        .astype(jnp.float32)
    )
    examples = 4 * owners
    example_hot = (
        rows_code.astype(jnp.float32)[:, None]
        == (jnp.arange(examples, dtype=jnp.float32) + 1.0)[None, :]
    ).astype(jnp.float32)
    spread = (example_hot[:, :, None] * proj_mine[:, None, :]).reshape(
        total_rows, examples * subs * slice_rank
    )
    grad_terms = lax.dot_general(
        spread,
        hidden_full,
        (((0,), (0,)), ((), ())),
        precision=lax.Precision.HIGHEST,
        preferred_element_type=jnp.float32,
    )
    grad_terms = grad_terms.reshape(examples, subs * slice_rank, rank_size)
    grad_blocks = lax.psum_scatter(
        grad_terms.astype(jnp.bfloat16), "sub", scatter_dimension=1, tiled=True
    ).astype(jnp.float32)
    grad_blocks = grad_blocks.reshape(examples, 1, slice_rank, rank_size)
    example_grads = lax.all_to_all(
        grad_blocks.astype(jnp.bfloat16), "expert", split_axis=0, concat_axis=1, tiled=True
    ).astype(grad_blocks.dtype)
    return (input_grad, example_grads)


def solution(mesh):
    return jax.shard_map(
        per_device,
        mesh=mesh,
        in_specs=(
            P(("groups", "expert", "sub", "pair"), None),
            P(("groups", "expert", "sub", "pair"), None),
            P(("groups", "expert", "sub", "pair"), None),
            P(("groups", "expert", "sub", "pair"), None),
            P(("groups", "expert", "sub", "pair")),
            P("expert", "sub", "pair"),
            P("expert", "sub", "pair"),
            P("expert", "pair", "sub"),
            P(),
            P(None, "pair"),
        ),
        out_specs=(
            P(("groups", "expert", "sub", "pair"), None),
            P(("groups", "expert"), None, ("sub", "pair"), None),
        ),
        check_vma=False,
    )
```

profile of v0, /device:TPU:0, one launch (start us, length us, event | category | flops | bytes accessed | tf_op | source)
XLA Modules:
  0.0 161.8 jit_solution(6309635558576419732)
XLA Ops:
  7.3 0.7 all-gather.11.cloned.1.call-update
  8.0 0.7 all-gather.9.cloned.1.call-update
  8.7 0.1 copy.64
  8.8 0.1 eq.66
  8.9 0.1 eq.62
  9.0 1.1 reduce-window.6
  10.2 0.2 slice_reduce_fusion
  10.4 0.2 reduce-window.9
  10.7 0.1 reshape.154
  10.9 0.1 fusion.13
  11.1 1.9 %all_gather.26 = bf16[2,4,10]{2,1,0:T(4,128)(2,1)S(1)} all-gather(bf16[1,4,10]{2,1,0:T(4,128)(2,1)S(1)} %broadcast_in_dim_reshape.15), channel_id=1, replica_groups=mesh['groups'=2,'expert'=4,'sub'=2,'pair'=2] {'pair'}, dimensions={0}, use_global_device_ids=true | all-gather | bytes 240 | tf_op jit(solution)/shard_map/all_gather | solution.py:51
  13.1 0.6 copy.74
  13.6 6.2 %all-to-all-start.3 = ((bf16[2,4,10]{2,0,1:T(2,128)(2,1)}), bf16[2,4,10]{2,0,1:T(2,128)(2,1)S(1)}, u32[]{:S(2)}, u32[]{:S(2)}) async-start(bf16[2,4,10]{2,0,1:T(2,128)(2,1)} %copy.74), calls=%async_computation.4 | async-start | bytes 4096 | tf_op jit(solution)/shard_map/all_to_all | solution.py:57
  19.8 0.7 all-gather.7.cloned.1.call-update
  20.7 0.1 copy.67
  20.8 0.1 reshape.152
  20.9 0.1 convolution_bitcast_fusion.1
  21.1 0.1 fusion.24
  21.2 0.2 fusion.3
  21.5 0.2 convolution_convert_fusion.5
  21.7 1.8 %all_gather.27 = bf16[2,4,10,64]{3,1,2,0:T(4,128)(2,1)S(1)} all-gather(bf16[1,4,10,64]{3,1,2,0:T(4,128)(2,1)S(1)} %copy.76), channel_id=1, replica_groups=mesh['groups'=2,'expert'=4,'sub'=2,'pair'=2] {'pair'}, dimensions={0}, use_global_device_ids=true | all-gather | bytes 15360 | tf_op jit(solution)/shard_map/all_gather | solution.py:52
  23.6 0.1 copy.68
  23.7 0.7 reshape.160
  24.4 0.9 all-to-all-done.3
  25.3 4.2 %all-to-all-start.4 = ((bf16[4,2,640]{2,1,0:T(2,128)(2,1)}), bf16[4,2,640]{2,1,0:T(2,128)(2,1)S(1)}, u32[]{:S(2)}, u32[]{:S(2)}) async-start(bf16[4,2,640]{2,1,0:T(2,128)(2,1)} %reshape.160), calls=%async_computation.5 | async-start | bytes 20480 | tf_op jit(solution)/shard_map/all_to_all | solution.py:58
  29.5 2.0 %all_gather.21 = bf16[2,4,10,2048]{3,1,2,0:T(4,128)(2,1)S(1)} all-gather(bf16[1,4,10,2048]{3,1,2,0:T(4,128)(2,1)S(1)} %copy.68), channel_id=1, replica_groups=mesh['groups'=2,'expert'=4,'sub'=2,'pair'=2] {'pair'}, dimensions={0}, use_global_device_ids=true | all-gather | bytes 491520 | tf_op jit(solution)/shard_map/all_gather | solution.py:50
  31.5 1.1 copy.69
  32.6 2.5 %all-to-all-done.4 = bf16[4,2,640]{2,1,0:T(2,128)(2,1)S(1)} async-done(((bf16[4,2,640]{2,1,0:T(2,128)(2,1)}), bf16[4,2,640]{2,1,0:T(2,128)(2,1)S(1)}, u32[]{:S(2)}, u32[]{:S(2)}) %all-to-all-start.4) | async-done | bytes 10272 | tf_op jit(solution)/shard_map/all_to_all | solution.py:58
  35.1 3.5 %all-to-all-start = ((bf16[2,4,10,2048]{3,0,2,1:T(2,128)(2,1)}), bf16[2,4,10,2048]{3,0,2,1:T(2,128)(2,1)S(1)}, u32[]{:S(2)}, u32[]{:S(2)}) async-start(bf16[2,4,10,2048]{3,0,2,1:T(2,128)(2,1)} %copy.69), calls=%async_computation | async-start | bytes 655360 | tf_op jit(solution)/shard_map/all_to_all | solution.py:56
  38.6 0.2 convolution_convert_fusion.1
  38.9 0.1 copy.71
  39.0 2.0 %all_gather.23 = bf16[2,4,10,2048]{3,1,2,0:T(4,128)(2,1)S(1)} all-gather(bf16[1,4,10,2048]{3,1,2,0:T(4,128)(2,1)S(1)} %copy.71), channel_id=1, replica_groups=mesh['groups'=2,'expert'=4,'sub'=2,'pair'=2] {'pair'}, dimensions={0}, use_global_device_ids=true | all-gather | bytes 491520 | tf_op jit(solution)/shard_map/all_gather | solution.py:49
  41.0 1.1 copy.72
  42.2 6.1 %all-to-all-done = bf16[2,4,10,2048]{3,0,2,1:T(2,128)(2,1)S(1)} async-done(((bf16[2,4,10,2048]{3,0,2,1:T(2,128)(2,1)}), bf16[2,4,10,2048]{3,0,2,1:T(2,128)(2,1)S(1)}, u32[]{:S(2)}, u32[]{:S(2)}) %all-to-all-start) | async-done | bytes 327712 | tf_op jit(solution)/shard_map/all_to_all | solution.py:56
  48.3 3.5 %all-to-all-start.1 = ((bf16[2,4,10,2048]{3,0,2,1:T(2,128)(2,1)}), bf16[2,4,10,2048]{3,0,2,1:T(2,128)(2,1)S(1)}, u32[]{:S(2)}, u32[]{:S(2)}) async-start(bf16[2,4,10,2048]{3,0,2,1:T(2,128)(2,1)} %copy.72), calls=%async_computation.1 | async-start | bytes 655360 | tf_op jit(solution)/shard_map/all_to_all | solution.py:55
  51.9 0.1 reshape.161
  52.0 0.1 reshape_reshape.3
  52.1 0.1 constant_dynamic-slice_fusion
  52.3 0.1 copy.70
  52.4 0.1 reshape.141
  52.5 7.8 %all-to-all-done.1 = bf16[2,4,10,2048]{3,0,2,1:T(2,128)(2,1)S(1)} async-done(((bf16[2,4,10,2048]{3,0,2,1:T(2,128)(2,1)}), bf16[2,4,10,2048]{3,0,2,1:T(2,128)(2,1)S(1)}, u32[]{:S(2)}, u32[]{:S(2)}) %all-to-all-start.1) | async-done | bytes 327712 | tf_op jit(solution)/shard_map/all_to_all | solution.py:55
  60.4 0.1 copy.73
  60.5 0.1 reshape.142
  60.7 2.1 %fusion.6 = f32[80,512]{1,0:T(8,128)S(1)} fusion(bf16[80,2048]{1,0:T(8,128)(2,1)S(1)} %reshape.142, bf16[1,2048,512]{2,1,0:T(8,128)(2,1)} %all-gather.11.cloned.1.call-done), kind=kOutput, calls=%fused_computation.10 | convolution fusion | flops 167772160 | bytes 2588672 | tf_op jit(solution)/shard_map/dot_general | solution.py:73
  62.8 17.4 %all-gather.9.cloned.1.call-done = bf16[1,2048,512]{2,1,0:T(8,128)(2,1)} async-done(((bf16[1,1024,512]{2,1,0:T(8,128)(2,1)}), bf16[1,2048,512]{2,1,0:T(8,128)(2,1)}) %all-gather.9.cloned.1.call-update) | async-done | bytes 2097168 | tf_op jit(solution)/shard_map/all_gather | solution.py:62
  80.2 2.1 %fusion.9 = f32[80,512]{1,0:T(8,128)S(1)} fusion(bf16[80,2048]{1,0:T(8,128)(2,1)S(1)} %reshape.142, bf16[1,2048,512]{2,1,0:T(8,128)(2,1)} %all-gather.9.cloned.1.call-done), kind=kOutput, calls=%fused_computation.13 | convolution fusion | flops 167772160 | bytes 2588672 | tf_op jit(solution)/shard_map/dot_general | solution.py:74
  82.2 0.2 convolution_convert_fusion.4
  82.4 3.5 %psum.7 = bf16[80,64]{0,1:T(8,128)(2,1)S(1)} all-reduce(bf16[80,64]{0,1:T(8,128)(2,1)S(1)} %convolution_convert_fusion.4), channel_id=1, replica_groups=mesh['groups'=2,'expert'=4,'sub'=2,'pair'=2] {'pair'}, use_global_device_ids=true, to_apply=%region_5.6 | all-reduce | flops 5120 | bytes 20480 | tf_op jit(solution)/shard_map/psum | solution.py:104
  85.9 0.9 convolution_convert_fusion.3
  86.9 27.9 %all-gather.7.cloned.1.call-done = bf16[1,512,2048]{2,1,0:T(8,128)(2,1)} async-done(((bf16[1,512,1024]{2,1,0:T(8,128)(2,1)}), bf16[1,512,2048]{2,1,0:T(8,128)(2,1)}) %all-gather.7.cloned.1.call-update) | async-done | bytes 2097168 | tf_op jit(solution)/shard_map/all_gather | solution.py:63
  114.9 2.4 %fusion.11 = f32[80,512]{1,0:T(8,128)S(1)} fusion(bf16[80,2048]{1,0:T(8,128)(2,1)S(1)} %reshape.141, bf16[1,512,2048]{2,1,0:T(8,128)(2,1)} %all-gather.7.cloned.1.call-done), kind=kOutput, calls=%fused_computation.15 | convolution fusion | flops 167772160 | bytes 2588672 | tf_op jit(solution)/shard_map/dot_general | solution.py:78
  117.2 0.8 fusion.4
  118.0 0.8 copy-done.2
  118.8 1.5 fusion
  120.3 7.4 %reduce-scatter.5.cloned.1.call-done = bf16[16,16,64]{2,1,0:T(8,128)(2,1)} async-done(((bf16[16,32,64]{2,1,0:T(8,128)(2,1)}), bf16[16,16,64]{2,1,0:T(8,128)(2,1)}) %reduce-scatter.5.cloned.1.call-update) | async-done | bytes 32784 | tf_op jit(solution)/shard_map/reduce_scatter | solution.py:128
  127.8 1.6 reshape.162
  129.3 4.6 %all-to-all-start.5 = ((bf16[4,2,2048]{2,1,0:T(2,128)(2,1)}), bf16[4,2,2048]{2,1,0:T(2,128)(2,1)S(1)}, u32[]{:S(2)}, u32[]{:S(2)}) async-start(bf16[4,2,2048]{2,1,0:T(2,128)(2,1)} %reshape.162), calls=%async_computation.7 | async-start | bytes 65536 | tf_op jit(solution)/shard_map/all_to_all | solution.py:132
  133.9 4.2 %reduce-scatter.3.cloned.1.call-done = bf16[40,2048]{1,0:T(8,128)(2,1)} async-done(((bf16[80,2048]{1,0:T(8,128)(2,1)}), bf16[40,2048]{1,0:T(8,128)(2,1)}) %reduce-scatter.3.cloned.1.call-update) | async-done | bytes 163856 | tf_op jit(solution)/shard_map/reduce_scatter | solution.py:91
  138.2 1.7 %reshape.143 = bf16[4,10,2048]{2,1,0:T(8,128)(2,1)} reshape(bf16[40,2048]{1,0:T(8,128)(2,1)} %reduce-scatter.3.cloned.1.call-done) | data formatting | bytes 327680 | tf_op jit(solution)/shard_map/reshape | solution.py:94
  139.9 4.9 %all-to-all-start.2 = ((bf16[4,10,2048]{2,1,0:T(8,128)(2,1)}), bf16[4,10,2048]{2,1,0:T(8,128)(2,1)S(1)}, u32[]{:S(2)}, u32[]{:S(2)}) async-start(bf16[4,10,2048]{2,1,0:T(8,128)(2,1)} %reshape.143), calls=%async_computation.3 | async-start | bytes 524288 | tf_op jit(solution)/shard_map/all_to_all | solution.py:95
  144.7 0.1 reshape.163
  144.8 0.7 copy_bitcast_fusion
  145.5 8.6 %all-to-all-done.2 = bf16[4,10,2048]{2,1,0:T(8,128)(2,1)S(1)} async-done(((bf16[4,10,2048]{2,1,0:T(8,128)(2,1)}), bf16[4,10,2048]{2,1,0:T(8,128)(2,1)S(1)}, u32[]{:S(2)}, u32[]{:S(2)}) %all-to-all-start.2) | async-done | bytes 163872 | tf_op jit(solution)/shard_map/all_to_all | solution.py:95
  154.1 1.1 convolution_convert_fusion
  (52 shorter events, 1.2 us)
Async XLA Ops:
  7.2 14.0 %copy-start = (bf16[128,2048]{1,0:T(8,128)(2,1)S(1)}, bf16[128,2048]{1,0:T(8,128)(2,1)}, u32[]{:S(2)}) copy-start(bf16[128,2048]{1,0:T(8,128)(2,1)} %param.11) | copy-start | bytes 1572868
  7.2 1.5 copy-start.5
  7.2 3.4 %copy-start.8 = (s32[128]{0:T(128)S(1)}, s32[128]{0:T(128)}, u32[]{:S(2)}) copy-start(s32[128]{0:T(128)} %param.14) | copy-start | bytes 1540
  7.2 13.5 %copy-start.6 = (bf16[128,8]{0,1:T(8,128)(2,1)S(1)}, bf16[128,8]{0,1:T(8,128)(2,1)}, u32[]{:S(2)}) copy-start(bf16[128,8]{0,1:T(8,128)(2,1)} %param.13) | copy-start | bytes 6148
  7.2 53.5 %all-gather.11.cloned.1.call-start = ((), (), s32[]{:S(2)}) async-start(), calls=%async_computation.12 | async-start | bytes 3145728 | tf_op jit(solution)/shard_map/all_gather | solution.py:61
  7.9 13.5 %copy-start.4 = (bf16[64,2048]{1,0:T(8,128)(2,1)S(1)}, bf16[64,2048]{1,0:T(8,128)(2,1)}, u32[]{:S(2)}) copy-start(bf16[64,2048]{1,0:T(8,128)(2,1)} %param.18) | copy-start | bytes 786436
  8.0 72.2 %all-gather.9.cloned.1.call-start = ((), (), s32[]{:S(2)}) async-start(), calls=%async_computation.11 | async-start | bytes 3145728 | tf_op jit(solution)/shard_map/all_gather | solution.py:62
  13.6 11.7 %all-to-all-start.3 = ((bf16[2,4,10]{2,0,1:T(2,128)(2,1)}), bf16[2,4,10]{2,0,1:T(2,128)(2,1)S(1)}, u32[]{:S(2)}, u32[]{:S(2)}) async-start(bf16[2,4,10]{2,0,1:T(2,128)(2,1)} %copy.74), calls=%async_computation.4 | async-start | bytes 4096 | tf_op jit(solution)/shard_map/all_to_all | solution.py:57
  19.8 95.0 %all-gather.7.cloned.1.call-start = ((), (), s32[]{:S(2)}) async-start(), calls=%async_computation.10 | async-start | bytes 3145728 | tf_op jit(solution)/shard_map/all_gather | solution.py:63
  20.8 17.8 %copy-start.3 = (bf16[128,2048]{1,0:T(8,128)(2,1)S(1)}, bf16[128,2048]{1,0:T(8,128)(2,1)}, u32[]{:S(2)}) copy-start(bf16[128,2048]{1,0:T(8,128)(2,1)} %param.10) | copy-start | bytes 1572868
  25.3 9.8 %all-to-all-start.4 = ((bf16[4,2,640]{2,1,0:T(2,128)(2,1)}), bf16[4,2,640]{2,1,0:T(2,128)(2,1)S(1)}, u32[]{:S(2)}, u32[]{:S(2)}) async-start(bf16[4,2,640]{2,1,0:T(2,128)(2,1)} %reshape.160), calls=%async_computation.5 | async-start | bytes 20480 | tf_op jit(solution)/shard_map/all_to_all | solution.py:58
  35.1 13.2 %all-to-all-start = ((bf16[2,4,10,2048]{3,0,2,1:T(2,128)(2,1)}), bf16[2,4,10,2048]{3,0,2,1:T(2,128)(2,1)S(1)}, u32[]{:S(2)}, u32[]{:S(2)}) async-start(bf16[2,4,10,2048]{3,0,2,1:T(2,128)(2,1)} %copy.69), calls=%async_computation | async-start | bytes 655360 | tf_op jit(solution)/shard_map/all_to_all | solution.py:56
  48.3 12.1 %all-to-all-start.1 = ((bf16[2,4,10,2048]{3,0,2,1:T(2,128)(2,1)}), bf16[2,4,10,2048]{3,0,2,1:T(2,128)(2,1)S(1)}, u32[]{:S(2)}, u32[]{:S(2)}) async-start(bf16[2,4,10,2048]{3,0,2,1:T(2,128)(2,1)} %copy.72), calls=%async_computation.1 | async-start | bytes 655360 | tf_op jit(solution)/shard_map/all_to_all | solution.py:55
  51.7 76.0 %reduce-scatter.5.cloned.1.call-start = ((), (), s32[]{:S(2)}) async-start(), calls=%async_computation.9 | async-start | bytes 196608 | tf_op jit(solution)/shard_map/reduce_scatter | solution.py:128
  60.7 21.6 %copy-start.7 = (bf16[64,512]{1,0:T(8,128)(2,1)S(1)}, bf16[64,512]{1,0:T(8,128)(2,1)}, u32[]{:S(2)}) copy-start(bf16[64,512]{1,0:T(8,128)(2,1)} %param.19) | copy-start | bytes 196612
  82.2 35.0 %copy-start.1 = (bf16[1,2048,512]{2,1,0:T(8,128)(2,1)S(1)}, bf16[1,2048,512]{2,1,0:T(8,128)(2,1)}, u32[]{:S(2)}) copy-start(bf16[1,2048,512]{2,1,0:T(8,128)(2,1)} %all-gather.11.cloned.1.call-done) | copy-start | bytes 6291460
  86.9 51.3 %reduce-scatter.3.cloned.1.call-start = ((), (), s32[]{:S(2)}) async-start(), calls=%async_computation.8 | async-start | bytes 491520 | tf_op jit(solution)/shard_map/reduce_scatter | solution.py:91
  117.2 1.6 copy-start.2
  129.3 10.5 %all-to-all-start.5 = ((bf16[4,2,2048]{2,1,0:T(2,128)(2,1)}), bf16[4,2,2048]{2,1,0:T(2,128)(2,1)S(1)}, u32[]{:S(2)}, u32[]{:S(2)}) async-start(bf16[4,2,2048]{2,1,0:T(2,128)(2,1)} %reshape.162), calls=%async_computation.7 | async-start | bytes 65536 | tf_op jit(solution)/shard_map/all_to_all | solution.py:132
  139.9 14.2 %all-to-all-start.2 = ((bf16[4,10,2048]{2,1,0:T(8,128)(2,1)}), bf16[4,10,2048]{2,1,0:T(8,128)(2,1)S(1)}, u32[]{:S(2)}, u32[]{:S(2)}) async-start(bf16[4,10,2048]{2,1,0:T(8,128)(2,1)} %reshape.143), calls=%async_computation.3 | async-start | bytes 524288 | tf_op jit(solution)/shard_map/all_to_all | solution.py:95
Sparse Core Ops, SparseCore 0:
  9.6 35.8 all-gather.10
  47.0 33.1 all-gather.8
  81.7 33.1 all-gather.6
  117.5 10.2 reduce-scatter.4
  130.4 7.7 reduce-scatter.2
where the time goes:
time: 163 us; the launch traced here: 162 us
  waiting for transfers between devices  85 us (52%)
  starting transfers between devices  26.9 us (17%)
  between operations  14.1 us (9%)
  matrix products  11.9 us (7%)
  blocking collectives  11.3 us (7%)
  local copies, waits for them, and re-layouts  10.2 us (6%)
  other arithmetic  2.33 us (1%)
    all_gather x1, waiting for transfers between devices, per_device(): lax.all_gather(down_w[0], 'sub', axis=1, tiled=True)  27.9 us
    all_gather x1, waiting for transfers between devices, per_device(): lax.all_gather(up_w[0], 'sub', axis=0, tiled=True)  17.4 us
    all_to_all x1, waiting for transfers between devices, per_device(): lax.all_to_all(summed, 'expert', split_axis=0, concat_axis=0, tiled=True)  8.57 us
    all_to_all x1, waiting for transfers between devices, per_device(): lax.all_to_all(grouped[0], 'expert', split_axis=1, concat_axis=1, tiled=T...  7.85 us
    reduce_scatter x1, waiting for transfers between devices, per_device(): lax.psum_scatter(grad_terms.astype(jnp.bfloat16), 'sub', scatter_dimensio...  7.45 us
    all_to_all x1, starting transfers between devices, per_device(): lax.all_to_all(grouped[2], 'expert', split_axis=1, concat_axis=1, tiled=T...  6.19 us
    all_to_all x1, waiting for transfers between devices, per_device(): lax.all_to_all(grouped[1], 'expert', split_axis=1, concat_axis=1, tiled=T...  6.08 us
    all_to_all x1, starting transfers between devices, per_device(): lax.all_to_all(summed, 'expert', split_axis=0, concat_axis=0, tiled=True)  4.85 us
  transfers between devices with their start and end apart: 11, of which 9 were waited for; matrix products, arithmetic and copies ran while one was open for 14% of the time, Pallas kernels for 0%

commit v1 on v0

v1 whole, which is shorter than its diff:
```python
import functools

import jax
import jax.numpy as jnp
from jax import lax
from jax.experimental import pallas as pl
from jax.experimental.pallas import tpu as pltpu
from jax.sharding import PartitionSpec as P

CAP = 10
PAD = 16
GROUP = 8
BLOCK = CAP * GROUP
LANES = 128
MESH = pl.DeviceIdType.MESH
F32 = jnp.float32
BF16 = jnp.bfloat16
NT = (((1,), (1,)), ((), ()))
TN = (((0,), (0,)), ((), ()))


def dot(a, b, dims=(((1,), (0,)), ((), ()))):
    return lax.dot_general(a, b, dims, preferred_element_type=F32)


def pack_matrix(rows, cols):
    i = lax.broadcasted_iota(jnp.int32, (rows, cols), 0)
    k = lax.broadcasted_iota(jnp.int32, (rows, cols), 1)
    hit = (k // PAD == i // CAP) & (k % PAD == i % CAP)
    return jnp.where(hit, 1.0, 0.0).astype(BF16)


def kernel(
    owners, subs, rank_size,
    payload, pick, gate, up, down, ph,
    out, eg_out,
    buf, comp, rs_send, rs_own, rs_buf, gbuf, hp_buf, rp, rp_in, ret_send, ret_buf, gs, eg_buf,
    d_send, d_recv, f_send, f_recv, rs_ss, rs_rs, g_ss, g_rs, h_ss, h_rs, p_ss, p_rs,
    r_ss, r_rs, e_ss, e_rs, l_sem,
):
    ei, si, pi = lax.axis_index("expert"), lax.axis_index("sub"), lax.axis_index("pair")
    other = 1 - pi
    sources = owners * subs
    me = ei * subs + si
    rows = comp.shape[0]
    half = rows // 2
    chunk = rows // subs
    wide = payload.shape[1] // subs
    dh = (wide - LANES) // 2
    ff = gate.shape[1]

    barrier = pltpu.get_barrier_semaphore()

    def greet(d, c):
        j = lax.rem(me + d, sources)
        pl.semaphore_signal(
            barrier, 1, device_id={"expert": j // subs, "sub": j % subs}, device_id_type=MESH
        )
        return c

    lax.fori_loop(1, sources, greet, 0)
    for d in range(subs):
        pl.semaphore_signal(
            barrier, 1, device_id={"sub": lax.rem(si + d, subs), "pair": other}, device_id_type=MESH
        )
    pl.semaphore_wait(barrier, sources - 1 + subs)

    def padded(j):
        return pl.ds(pl.multiple_of(j * PAD, PAD), PAD)

    def dispatch(d):
        j = lax.rem(me + d, sources)
        e, s = j // subs, j % subs
        return pltpu.make_async_remote_copy(
            src_ref=payload.at[padded(e), pl.ds(pl.multiple_of(s * wide, LANES), wide)],
            dst_ref=buf.at[pi, padded(me)],
            send_sem=d_send.at[j],
            recv_sem=d_recv.at[me],
            device_id={"expert": e, "sub": s},
            device_id_type=MESH,
        )

    def start_dispatch(d, c):
        dispatch(d).start()
        return c

    lax.fori_loop(1, sources, start_dispatch, 0)
    mine = payload.at[padded(ei), pl.ds(pl.multiple_of(si * wide, LANES), wide)]
    local = pltpu.make_async_copy(mine, buf.at[pi, padded(me)], l_sem)
    local.start()

    def arrived(j):
        return pltpu.make_async_remote_copy(
            src_ref=buf.at[pi, padded(j)],
            dst_ref=buf.at[pi, padded(j)],
            send_sem=d_send.at[j],
            recv_sem=d_recv.at[j],
            device_id={"expert": j // subs, "sub": j % subs},
            device_id_type=MESH,
        )

    def forward(j, half_at):
        return pltpu.make_async_remote_copy(
            src_ref=buf.at[half_at, padded(j)],
            dst_ref=buf.at[half_at, padded(j)],
            send_sem=f_send.at[j],
            recv_sem=f_recv.at[j],
            device_id={"pair": other},
            device_id_type=MESH,
        )

    local.wait()
    forward(me, pi).start()

    def pass_on(d, c):
        j = lax.rem(me - d + sources, sources)
        arrived(j).wait_recv()
        forward(j, pi).start()
        return c

    lax.fori_loop(1, sources, pass_on, 0)

    squeeze = pack_matrix(BLOCK, GROUP * PAD)

    def compact(half_at):
        def body(g, c):
            part = buf[half_at, pl.ds(pl.multiple_of(g * GROUP * PAD, GROUP * PAD), GROUP * PAD), :]
            at = pl.multiple_of(half_at * half + g * BLOCK, PAD)
            comp[pl.ds(at, BLOCK), :] = dot(squeeze, part).astype(BF16)
            return c

        lax.fori_loop(0, sources // GROUP, body, 0)

    compact(pi)

    def take_pass(j, c):
        forward(j, other).wait_recv()
        return c

    lax.fori_loop(0, sources, take_pass, 0)
    compact(other)

    def partial(at, store):
        x = comp[pl.ds(at, BLOCK), 0:dh]
        z = comp[pl.ds(at, BLOCK), dh : 2 * dh]
        store(0, dot(x, gate[...]))
        store(1, dot(x, up[...]))
        store(2, dot(z, down[...], NT))

    def rs_copy(d):
        s = lax.rem(si + d, subs)
        return pltpu.make_async_remote_copy(
            src_ref=rs_send.at[pl.ds(pl.multiple_of(s * chunk, PAD), chunk)],
            dst_ref=rs_buf.at[si],
            send_sem=rs_ss.at[s],
            recv_sem=rs_rs.at[si],
            device_id={"sub": s},
            device_id_type=MESH,
        )

    for d in range(1, subs):
        base = lax.rem(si + d, subs) * chunk

        def send_block(b, c):
            at = pl.multiple_of(base + b * BLOCK, PAD)

            def store(k, v):
                rs_send[pl.ds(at, BLOCK), k * ff : (k + 1) * ff] = v.astype(BF16)

            partial(at, store)
            return c

        lax.fori_loop(0, chunk // BLOCK, send_block, 0)
        rs_copy(d).start()

    def own_block(b, c):
        to = pl.multiple_of(b * BLOCK, PAD)

        def store(k, v):
            rs_own[pl.ds(to, BLOCK), k * ff : (k + 1) * ff] = v

        partial(pl.multiple_of(si * chunk + b * BLOCK, PAD), store)
        return c

    lax.fori_loop(0, chunk // BLOCK, own_block, 0)

    def rs_wait(d):
        s = lax.rem(si + d, subs)
        return pltpu.make_async_remote_copy(
            src_ref=rs_buf.at[s],
            dst_ref=rs_buf.at[s],
            send_sem=rs_ss.at[s],
            recv_sem=rs_rs.at[s],
            device_id={"sub": s},
            device_id_type=MESH,
        )

    for d in range(1, subs):
        rs_wait(d).wait_recv()

    hp_me = si * 2 + pi

    def act_block(b, c):
        to = pl.multiple_of(b * BLOCK, PAD)

        def total(k):
            v = rs_own[pl.ds(to, BLOCK), k * ff : (k + 1) * ff]
            for d in range(1, subs):
                s = lax.rem(si + d, subs)
                v = v + rs_buf[s, pl.ds(to, BLOCK), k * ff : (k + 1) * ff].astype(F32)
            return v

        g, u, h = total(0), total(1), total(2)
        sig = 1.0 / (1.0 + jnp.exp(-g))
        silu = g * sig
        at = pl.multiple_of(si * chunk + b * BLOCK, PAD)
        gbuf[pl.ds(at, BLOCK), 0:ff] = (h * u * sig * (1.0 + g * (1.0 - sig))).astype(BF16)
        gbuf[pl.ds(at, BLOCK), ff : 2 * ff] = (h * silu).astype(BF16)
        hp_buf[hp_me, pl.ds(to, BLOCK), :] = dot((silu * u).astype(BF16), ph[...], NT)
        return c

    lax.fori_loop(0, chunk // BLOCK, act_block, 0)

    def g_copy(d, came):
        s = lax.rem(si + d, subs)
        at = s if came else si
        span = gbuf.at[pl.ds(pl.multiple_of(at * chunk, PAD), chunk)]
        return pltpu.make_async_remote_copy(
            src_ref=span,
            dst_ref=span,
            send_sem=g_ss.at[s],
            recv_sem=g_rs.at[at],
            device_id={"sub": s},
            device_id_type=MESH,
        )

    def h_copy(d, came):
        q = lax.rem(hp_me + d, 2 * subs)
        at = q if came else hp_me
        return pltpu.make_async_remote_copy(
            src_ref=hp_buf.at[at],
            dst_ref=hp_buf.at[at],
            send_sem=h_ss.at[q],
            recv_sem=h_rs.at[at],
            device_id={"sub": q // 2, "pair": q % 2},
            device_id_type=MESH,
        )

    for d in range(1, subs):
        g_copy(d, False).start()
    for d in range(1, 2 * subs):
        h_copy(d, False).start()

    def route_chunk(s):
        def body(b, c):
            at = pl.multiple_of(s * chunk + b * BLOCK, PAD)
            v = dot(gbuf[pl.ds(at, BLOCK), 0:ff], gate[...], NT)
            v = v + dot(gbuf[pl.ds(at, BLOCK), ff : 2 * ff], up[...], NT)
            rp[pl.ds(at, BLOCK), :] = v.astype(BF16)
            return c

        lax.fori_loop(0, chunk // BLOCK, body, 0)

    route_chunk(si)
    for d in range(1, subs):
        g_copy(d, True).wait_recv()
        route_chunk(lax.rem(si + d, subs))

    swap = pltpu.make_async_remote_copy(
        src_ref=rp.at[pl.ds(pl.multiple_of(other * half, PAD), half)],
        dst_ref=rp_in,
        send_sem=p_ss,
        recv_sem=p_rs,
        device_id={"pair": other},
        device_id_type=MESH,
    )
    swap.start()
    swap.wait_recv()

    def sum_block(g, c):
        to = pl.multiple_of(g * BLOCK, PAD)
        at = pl.multiple_of(pi * half + g * BLOCK, PAD)
        v = rp[pl.ds(at, BLOCK), :].astype(F32) + rp_in[pl.ds(to, BLOCK), :].astype(F32)
        put = pl.multiple_of(g * GROUP * PAD, GROUP * PAD)
        ret_send[pl.ds(put, GROUP * PAD), :] = dot(squeeze, v.astype(BF16), TN).astype(BF16)
        return c

    lax.fori_loop(0, sources // GROUP, sum_block, 0)

    def back(j, came):
        at_e = j // subs if came else ei
        at_s = j % subs if came else si
        return pltpu.make_async_remote_copy(
            src_ref=ret_send.at[padded(j)],
            dst_ref=ret_buf.at[padded(at_e), pl.ds(pl.multiple_of(at_s * dh, LANES), dh)],
            send_sem=r_ss.at[j],
            recv_sem=r_rs.at[j if came else me],
            device_id={"expert": j // subs, "sub": j % subs},
            device_id_type=MESH,
        )

    def start_back(d, c):
        back(lax.rem(me + d, sources), False).start()
        return c

    lax.fori_loop(1, sources, start_back, 0)
    ret_buf[padded(ei), pl.ds(pl.multiple_of(si * dh, LANES), dh)] = ret_send[padded(me), :]

    for d in range(1, 2 * subs):
        h_copy(d, True).wait_recv()
    share = rank_size // (2 * subs)
    spread_cols = gs.shape[0]
    row = lax.broadcasted_iota(jnp.int32, (LANES, spread_cols), 0)
    col = lax.broadcasted_iota(jnp.int32, (LANES, spread_cols), 1)
    repeat = jnp.where(row == hp_me * share + col % share, 1.0, 0.0).astype(BF16)
    code_row = jnp.where(row == rank_size, 1.0, 0.0).astype(BF16)
    want = (
        lax.broadcasted_iota(jnp.int32, (BLOCK, spread_cols), 1) // share + 1
    ).astype(F32)

    def example_block(b, acc):
        at = pl.multiple_of(b * BLOCK, PAD)
        extra = comp[pl.ds(at, BLOCK), 2 * dh : wide]
        spread = jnp.where(dot(extra, code_row) == want, dot(extra, repeat), 0.0).astype(BF16)
        s = b // (chunk // BLOCK)
        to = pl.multiple_of((b % (chunk // BLOCK)) * BLOCK, PAD)
        hp = hp_buf[2 * s, pl.ds(to, BLOCK), :] + hp_buf[2 * s + 1, pl.ds(to, BLOCK), :]
        hi = hp.astype(BF16)
        rest = hp - hi.astype(F32)
        mid = rest.astype(BF16)
        low = (rest - mid.astype(F32)).astype(BF16)
        return acc + dot(spread, hi, TN) + dot(spread, mid, TN) + dot(spread, low, TN)

    gs[...] = lax.fori_loop(
        0, rows // BLOCK, example_block, jnp.zeros((spread_cols, LANES), F32)
    ).astype(BF16)
    piece = spread_cols // owners

    def e_copy(e, came):
        return pltpu.make_async_remote_copy(
            src_ref=gs.at[pl.ds(pl.multiple_of(e * piece, PAD), piece)],
            dst_ref=eg_buf.at[e if came else ei],
            send_sem=e_ss.at[e],
            recv_sem=e_rs.at[e if came else ei],
            device_id={"expert": e},
            device_id_type=MESH,
        )

    def start_e(d, c):
        e_copy(lax.rem(ei + d, owners), False).start()
        return c

    lax.fori_loop(1, owners, start_e, 0)
    eg_buf[ei] = gs[pl.ds(pl.multiple_of(ei * piece, PAD), piece), :]

    def take_back(d, c):
        back(lax.rem(me + d, sources), True).wait_recv()
        return c

    lax.fori_loop(1, sources, take_back, 0)
    out[...] = dot(pick[...], ret_buf[...], TN).astype(BF16)

    def take_e(d, c):
        e_copy(lax.rem(ei + d, owners), True).wait_recv()
        return c

    lax.fori_loop(1, owners, take_e, 0)
    eg_out[...] = eg_buf[...].astype(F32)

    def sent(d, c):
        j = lax.rem(me + d, sources)
        dispatch(d).wait_send()
        back(j, False).wait_send()
        return c

    lax.fori_loop(1, sources, sent, 0)

    def sent_pass(j, c):
        forward(j, pi).wait_send()
        return c

    lax.fori_loop(0, sources, sent_pass, 0)
    for d in range(1, subs):
        rs_copy(d).wait_send()
        g_copy(d, False).wait_send()
    for d in range(1, 2 * subs):
        h_copy(d, False).wait_send()
    swap.wait_send()

    def sent_e(d, c):
        e_copy(lax.rem(ei + d, owners), False).wait_send()
        return c

    lax.fori_loop(1, owners, sent_e, 0)


def per_device(
    tokens, out_grad, routes, route_weight, example_id, gate_w, up_w, down_w, proj_grad, proj_hidden
):
    owners = lax.axis_size("expert")
    subs = lax.axis_size("sub")
    local_tokens, width = tokens.shape
    fanout = routes.shape[1]
    rank_size = proj_grad.shape[0]
    slots = owners * PAD
    dh = width // subs
    wide = 2 * dh + LANES
    ff = gate_w.shape[2]
    sources = owners * subs
    rows = sources * 2 * CAP
    chunk = rows // subs
    examples = 4 * owners
    share = rank_size // (2 * subs)
    route_flat = routes.reshape(-1)
    inside = route_flat < owners
    named = (
        routes[:, :, None] == jnp.arange(owners, dtype=jnp.int32)[None, None, :]
    )
    taken = jnp.any(named, axis=1)
    order = (
        jnp.arange(local_tokens)[:, None] > jnp.arange(local_tokens)[None, :]
    ).astype(BF16)
    before = dot(order, taken.astype(BF16)).astype(jnp.int32)
    weight = jnp.sum(
        jnp.where(named, route_weight.astype(F32)[:, :, None], 0.0), axis=1
    )
    hit = (
        before.T[:, None, :] == jnp.arange(PAD, dtype=jnp.int32)[None, :, None]
    ) & taken.T[:, None, :]
    pick_token = hit.astype(BF16).reshape(slots, local_tokens)
    slot_weight = jnp.sum(jnp.where(hit, weight.T[:, None, :], 0.0), axis=2).reshape(slots)
    slot_code = jnp.sum(
        jnp.where(hit, (example_id + 1).astype(F32)[None, None, :], 0.0), axis=2
    ).reshape(slots)
    rows_in = dot(pick_token, tokens).astype(BF16)
    rows_grad = (slot_weight[:, None] * dot(pick_token, out_grad)).astype(BF16)
    slot_proj = dot(rows_grad, proj_grad, NT).astype(BF16)
    extra = jnp.concatenate(
        [
            slot_proj,
            slot_code.astype(BF16)[:, None],
            jnp.zeros((slots, LANES - rank_size - 1), BF16),
        ],
        axis=1,
    )
    parts = []
    for s in range(subs):
        parts += [rows_in[:, s * dh : (s + 1) * dh], rows_grad[:, s * dh : (s + 1) * dh], extra]
    payload = jnp.concatenate(parts, axis=1)
    ph = jnp.concatenate(
        [proj_hidden, jnp.zeros((LANES - rank_size, proj_hidden.shape[1]), BF16)], axis=0
    )
    vmem = pl.BlockSpec(memory_space=pltpu.VMEM)
    dma = pltpu.SemaphoreType.DMA
    piece = 4 * share
    input_grad, eg = pl.pallas_call(
        functools.partial(kernel, owners, subs, rank_size),
        out_shape=(
            jax.ShapeDtypeStruct((local_tokens, width), BF16),
            jax.ShapeDtypeStruct((owners, piece, LANES), F32),
        ),
        in_specs=[vmem] * 6,
        out_specs=(vmem, vmem),
        scratch_shapes=[
            pltpu.VMEM((2, sources * PAD, wide), BF16),
            pltpu.VMEM((rows, wide), BF16),
            pltpu.VMEM((rows, 3 * ff), BF16),
            pltpu.VMEM((chunk, 3 * ff), F32),
            pltpu.VMEM((subs, chunk, 3 * ff), BF16),
            pltpu.VMEM((rows, 2 * ff), BF16),
            pltpu.VMEM((2 * subs, chunk, LANES), F32),
            pltpu.VMEM((rows, dh), BF16),
            pltpu.VMEM((rows // 2, dh), BF16),
            pltpu.VMEM((sources * PAD, dh), BF16),
            pltpu.VMEM((slots, width), BF16),
            pltpu.VMEM((examples * share, LANES), BF16),
            pltpu.VMEM((owners, piece, LANES), BF16),
            dma((sources,)), dma((sources,)), dma((sources,)), dma((sources,)),
            dma((subs,)), dma((subs,)), dma((subs,)), dma((subs,)),
            dma((2 * subs,)), dma((2 * subs,)), dma(()), dma(()),
            dma((sources,)), dma((sources,)), dma((owners,)), dma((owners,)), dma(()),
        ],
        compiler_params=pltpu.CompilerParams(
            collective_id=0, has_side_effects=True, vmem_limit_bytes=60 * 1024 * 1024
        ),
    )(payload, pick_token, gate_w[0], up_w[0], down_w[0], ph)
    eg = eg.reshape(owners, 4, share, LANES)[..., :rank_size]
    return (input_grad, jnp.swapaxes(eg, 0, 1))


def solution(mesh):
    return jax.shard_map(
        per_device,
        mesh=mesh,
        in_specs=(
            P(("groups", "expert", "sub", "pair"), None),
            P(("groups", "expert", "sub", "pair"), None),
            P(("groups", "expert", "sub", "pair"), None),
            P(("groups", "expert", "sub", "pair"), None),
            P(("groups", "expert", "sub", "pair")),
            P("expert", "sub", "pair"),
            P("expert", "sub", "pair"),
            P("expert", "pair", "sub"),
            P(),
            P(None, "pair"),
        ),
        out_specs=(
            P(("groups", "expert", "sub", "pair"), None),
            P(("groups", "expert"), None, ("sub", "pair"), None),
        ),
        check_vma=False,
    )
```

time: 163 us -> 57.3 us (0.35)
  waiting for transfers between devices: 85 us -> 0 us
  Pallas kernels: 0 us -> 46.4 us
  starting transfers between devices: 26.9 us -> 0 us
  between operations: 14.1 us -> 0.72 us
  blocking collectives: 11.3 us -> 0 us
  matrix products: 11.9 us -> 0.79 us
  local copies, waits for them, and re-layouts: 10.2 us -> 6.86 us
    pallas_call x0 -> x1, Pallas kernels: none -> 46.4 us  [per_device(): pl.pallas_call(functools.partial(kernel, owners, subs, rank_size), out_sh...]
    all_gather x3 -> x0, waiting for transfers between devices: 45.3 us -> none  [the longest x1 27.9 us: per_device(): lax.all_gather(down_w[0], 'sub', axis=1, tiled=True)]
    all_to_all x6 -> x0, starting transfers between devices: 26.8 us -> none  [the longest x1 6.19 us: per_device(): lax.all_to_all(grouped[2], 'expert', split_axis=1, concat_axis=1, tiled=T...]
    all_to_all x6 -> x0, waiting for transfers between devices: 25.9 us -> none  [the longest x1 8.57 us: per_device(): lax.all_to_all(summed, 'expert', split_axis=0, concat_axis=0, tiled=True)]
    reduce_scatter x2 -> x0, waiting for transfers between devices: 11.7 us -> none  [the longest x1 7.45 us: per_device(): lax.psum_scatter(grad_terms.astype(jnp.bfloat16), 'sub', scatter_dimensio...]
    dot_general x13 -> x4, matrix products: 11.9 us -> 0.79 us  [dot(): return lax.dot_general(a, b, dims, preferred_element_type=F32)]
    all_gather x4 -> x0, blocking collectives: 7.8 us -> none  [the longest x1 2.04 us: per_device(): lax.all_gather(rows_in[None], 'pair', axis=0, tiled=True)]
    psum x1 -> x0, blocking collectives: 3.49 us -> none  [per_device(): lax.psum(hidden_part.astype(jnp.bfloat16), 'pair').astype(jnp.float32)]
  transfers between devices with their start and end apart: 11 -> 0, of which waited for: 9 -> 0; matrix products, arithmetic and copies ran while one was open for 14% -> 0% of each run, Pallas kernels for 0% -> 0%
where the time goes in v1:
time: 57.3 us; the launch traced here: 57 us
  Pallas kernels  46.4 us (81%)
  local copies, waits for them, and re-layouts  6.86 us (12%)
  other arithmetic  2.19 us (4%)
  matrix products  0.79 us (1%)
  between operations  0.72 us (1%)
    pallas_call x1, Pallas kernels, per_device(): pl.pallas_call(functools.partial(kernel, owners, subs, rank_size), out_sh...  46.4 us
    unnamed x11, local copies, waits for them, and re-layouts  3.35 us
    transpose x1, local copies, waits for them, and re-layouts, per_device(): return (input_grad, jnp.swapaxes(eg, 0, 1))  1.57 us

profile of v1, /device:TPU:0, one launch (start us, length us, event | category | flops | bytes accessed | tf_op | source)
XLA Modules:
  0.0 57.0 jit_solution(9003401497453531449)
XLA Ops:
  0.6 0.0 copy-start
  0.6 0.0 copy-start.4
  0.7 0.0 copy-start.3
  0.7 0.7 %copy-done.4 = s32[128,8]{0,1:T(8,128)S(1)} copy-done((s32[128,8]{0,1:T(8,128)S(1)}, s32[128,8]{0,1:T(8,128)}, u32[]{:S(2)}) %copy-start.4) | copy-done | bytes 4120
  1.4 0.7 %add_convert_fusion = f32[128]{0:T(128)S(1)} fusion(s32[128]{0:T(128)} %param.14), kind=kLoop, calls=%fused_computation.16 | loop fusion | flops 256 | bytes 1024 | tf_op jit(solution)/shard_map/convert_element_type | solution.py:433
  2.1 0.1 convolution_convert_fusion.2
  2.2 0.1 eq.44
  2.3 0.7 %convert_element_type.40 = f32[128,8]{0,1:T(8,128)S(1)} convert(bf16[128,8]{0,1:T(8,128)(2,1)} %param.13) | non-fusion elementwise | flops 1024 | bytes 6144 | tf_op jit(solution)/shard_map/convert_element_type | solution.py:425
  3.0 0.1 select_reduce_fusion
  3.1 0.1 mul.10
  3.2 0.1 convert_element_type.47
  3.3 0.7 %fusion.4 = (bf16[64,128]{1,0:T(8,128)(2,1)}, pred[64,128]{1,0:T(32,128)(4,1)S(1)}) fusion(pred[4,128]{1,0:T(4,128)(4,1)S(1)} %bitcast.31, s32[64]{0:T(128)S(1)} %eq.44, s32[4,128]{1,0:T(4,128)S(1)} %convolution_convert_fusion.2), kind=kLoop, calls=%fused_computation.17 | loop fusion | flops 24576 | bytes 27392 | tf_op jit(solution)/shard_map/convert_element_type | solution.py:430
  4.0 0.0 copy-done.3
  4.0 0.7 %concatenate.9.ph = bf16[128,512]{1,0:T(8,128)(2,1)} pad(bf16[64,512]{1,0:T(8,128)(2,1)S(1)} %copy-done.3, bf16[]{:T(256)} %constant.2.clone.1), padding=0_64x0_0 | pad | bytes 196610 | tf_op jit(solution)/shard_map/concatenate | solution.py:450
  4.7 0.0 copy-done
  4.7 0.0 copy-start.2
  4.7 0.0 copy-start.1
  4.7 0.2 fusion
  4.9 0.7 %copy-done.2 = bf16[64,2048]{1,0:T(8,128)(2,1)S(1)} copy-done((bf16[64,2048]{1,0:T(8,128)(2,1)S(1)}, bf16[64,2048]{1,0:T(8,128)(2,1)}, u32[]{:S(2)}) %copy-start.2) | copy-done | bytes 262168
  5.6 0.2 convolution_convert_fusion.1
  5.8 0.0 copy-done.1
  5.9 0.2 convolution_convert_fusion
  6.1 1.0 %concatenate.8.payload = bf16[64,4352]{1,0:T(8,128)(2,1)} concatenate(bf16[64,1024]{1,0:T(8,128)(2,1)S(1)} %get-tuple-element.14, bf16[64,1024]{1,0:T(8,128)(2,1)S(1)} %get-tuple-element.9, bf16[64,64]{1,0:T(8,128)(2,1)S(1)} %convolution_convert_fusion.1, bf16[64,1]{1,0:T(8,128)(2,1)S(1)} %convert_element_type.47, bf16[64,63]{1,0:T(8,128)(2,1)S(1)} %broadcast_in_dim.54, ...), dimensions={1} | concatenate | bytes 1114112 | tf_op jit(solution)/shard_map/concatenate | solution.py:449
  7.1 46.4 %shard_map.113 = (bf16[128,2048]{1,0:T(8,128)(2,1)}, f32[4,64,128]{2,1,0:T(8,128)}) custom-call(bf16[64,4352]{1,0:T(8,128)(2,1)} %concatenate.8.payload, bf16[64,128]{1,0:T(8,128)(2,1)} %get-tuple-element.12.pick, bf16[1024,512]{1,0:T(8,128)(2,1)} %bitcast.25, bf16[1024,512]{1,0:T(8,128)(2,1)} %bitcast.26, bf16[512,1024]{1,0:T(8,128)(2,1)} %bitcast.27, ...), custom_call_target="tpu_custom_call" | custom-call | tf_op jit(solution)/shard_map/pallas_call | solution.py:456
  53.5 1.6 %copy_bitcast_fusion = f32[4,4,16,64]{3,2,1,0:T(8,128)} fusion(f32[4,4,16,128]{3,2,1,0:T(8,128)} %bitcast.28), kind=kLoop, calls=%fused_computation.5 | loop fusion | bytes 196608 | tf_op jit(solution)/shard_map/transpose | solution.py:488
  55.1 1.9 %copy.26 = bf16[128,2048]{1,0:T(8,128)(2,1)} copy(bf16[128,2048]{1,0:T(8,128)(2,1)} %get-tuple-element.18) | data formatting | bytes 1048576
  (5 shorter events, 0.1 us)
Async XLA Ops:
  0.6 4.0 %copy-start = (bf16[128,2048]{1,0:T(8,128)(2,1)S(1)}, bf16[128,2048]{1,0:T(8,128)(2,1)}, u32[]{:S(2)}) copy-start(bf16[128,2048]{1,0:T(8,128)(2,1)} %param.11) | copy-start | bytes 1572868
  0.6 0.7 %copy-start.4 = (s32[128,8]{0,1:T(8,128)S(1)}, s32[128,8]{0,1:T(8,128)}, u32[]{:S(2)}) copy-start(s32[128,8]{0,1:T(8,128)} %param.12) | copy-start | bytes 12292
  0.7 3.3 %copy-start.3 = (bf16[64,512]{1,0:T(8,128)(2,1)S(1)}, bf16[64,512]{1,0:T(8,128)(2,1)}, u32[]{:S(2)}) copy-start(bf16[64,512]{1,0:T(8,128)(2,1)} %param.19) | copy-start | bytes 196612
  4.7 1.0 %copy-start.2 = (bf16[64,2048]{1,0:T(8,128)(2,1)S(1)}, bf16[64,2048]{1,0:T(8,128)(2,1)}, u32[]{:S(2)}) copy-start(bf16[64,2048]{1,0:T(8,128)(2,1)} %param.18) | copy-start | bytes 786436
  4.7 1.2 %copy-start.1 = (bf16[128,2048]{1,0:T(8,128)(2,1)S(1)}, bf16[128,2048]{1,0:T(8,128)(2,1)}, u32[]{:S(2)}) copy-start(bf16[128,2048]{1,0:T(8,128)(2,1)} %param.10) | copy-start | bytes 1572868

commit v2 on v1

v2 whole, which is shorter than its diff:
```python
import functools

import jax
import jax.numpy as jnp
from jax import lax
from jax.experimental import pallas as pl
from jax.experimental.pallas import tpu as pltpu
from jax.sharding import PartitionSpec as P

CAP = 10
PAD = 16
GROUP = 8
BLOCK = CAP * GROUP
LANES = 128
MESH = pl.DeviceIdType.MESH
F32 = jnp.float32
BF16 = jnp.bfloat16
NT = (((1,), (1,)), ((), ()))
TN = (((0,), (0,)), ((), ()))


def dot(a, b, dims=(((1,), (0,)), ((), ()))):
    return lax.dot_general(a, b, dims, preferred_element_type=F32)


def pack_matrix(rows, cols):
    i = lax.broadcasted_iota(jnp.int32, (rows, cols), 0)
    k = lax.broadcasted_iota(jnp.int32, (rows, cols), 1)
    hit = (k // PAD == i // CAP) & (k % PAD == i % CAP)
    return jnp.where(hit, 1.0, 0.0).astype(BF16)


def kernel(
    owners, subs, rank_size,
    routes_t, weight_t, example, tokens, out_grad, gate_in, up_in, down_in, proj, ph,
    ret_out, pick_out, eg_out,
    tok, og, gate, up, down, pj, px, pz, bufx, bufz, compx, compz,
    gu_send, gu_own, gu_buf, hg_send, hg_own, hg_buf, gbuf, hp_buf, rp_in, ret_buf,
    gs, eg_buf,
    load_sem, x_send, x_recv, z_send, z_recv, fx_send, fx_recv, fz_send, fz_recv,
    gu_ss, gu_rs, hg_ss, hg_rs, g_ss, g_rs, h_ss, h_rs, p_ss, p_rs, r_ss, r_rs, e_ss, e_rs,
):
    ei, si, pi = lax.axis_index("expert"), lax.axis_index("sub"), lax.axis_index("pair")
    other = 1 - pi
    sources = owners * subs
    me = ei * subs + si
    rows = compx.shape[0]
    half = rows // 2
    chunk = rows // subs
    dh = compx.shape[1]
    zw = compz.shape[1]
    ff = gate.shape[1]

    loads = [
        pltpu.make_async_copy(a, b, load_sem.at[k])
        for k, (a, b) in enumerate(
            [(tokens, tok), (out_grad, og), (proj, pj), (gate_in, gate), (up_in, up), (down_in, down)]
        )
    ]
    for load in loads:
        load.start()

    barrier = pltpu.get_barrier_semaphore()

    def greet(d, c):
        j = lax.rem(me + d, sources)
        pl.semaphore_signal(
            barrier, 1, device_id={"expert": j // subs, "sub": j % subs}, device_id_type=MESH
        )
        return c

    lax.fori_loop(1, sources, greet, 0)
    for d in range(subs):
        pl.semaphore_signal(
            barrier, 1, device_id={"sub": lax.rem(si + d, subs), "pair": other}, device_id_type=MESH
        )

    tokens_here = tok.shape[0]
    named = [(routes_t[...] == e) for e in range(owners)]
    taken = jnp.concatenate(
        [jnp.sum(jnp.where(n, 1.0, 0.0), axis=0, keepdims=True) for n in named], axis=0
    )
    weights = weight_t[...].astype(F32)
    chosen = [jnp.sum(jnp.where(n, weights, 0.0), axis=0, keepdims=True) for n in named]
    lower = lax.broadcasted_iota(jnp.int32, (tokens_here, tokens_here), 0)
    upper = lax.broadcasted_iota(jnp.int32, (tokens_here, tokens_here), 1)
    before = dot(taken.astype(BF16), jnp.where(lower < upper, 1.0, 0.0).astype(BF16))
    slot = lax.broadcasted_iota(jnp.int32, (PAD, tokens_here), 0).astype(F32)
    hits, slot_weights, slot_codes = [], [], []
    codes = (example[...] + 1).astype(F32)
    for e in range(owners):
        hit = jnp.where((before[e : e + 1] == slot) & (taken[e : e + 1] > 0.5), 1.0, 0.0)
        hits.append(hit)
        slot_weights.append(jnp.sum(hit * chosen[e], axis=1, keepdims=True))
        slot_codes.append(jnp.sum(hit * codes, axis=1, keepdims=True))
    pick = jnp.concatenate(hits, axis=0).astype(BF16)
    slot_weight = jnp.concatenate(slot_weights, axis=0)
    slot_code = jnp.concatenate(slot_codes, axis=0)
    pick_out[...] = pick
    loads[0].wait()
    px[...] = dot(pick, tok[...]).astype(BF16)
    pl.semaphore_wait(barrier, sources - 1 + subs)

    def padded(j):
        return pl.ds(pl.multiple_of(j * PAD, PAD), PAD)

    def rows_to(d, pack, buf, ss, rs):
        j = lax.rem(me + d, sources)
        e, s = j // subs, j % subs
        wide = buf.shape[2]
        return pltpu.make_async_remote_copy(
            src_ref=pack.at[padded(e), pl.ds(pl.multiple_of(s * wide, LANES), wide)],
            dst_ref=buf.at[pi, padded(me)],
            send_sem=ss.at[j],
            recv_sem=rs.at[me],
            device_id={"expert": e, "sub": s},
            device_id_type=MESH,
        )

    def forward(j, half_at, buf, ss, rs):
        return pltpu.make_async_remote_copy(
            src_ref=buf.at[half_at, padded(j)],
            dst_ref=buf.at[half_at, padded(j)],
            send_sem=ss.at[j],
            recv_sem=rs.at[j],
            device_id={"pair": other},
            device_id_type=MESH,
        )

    def send_rows(pack, buf, ss, rs, fss, frs):
        def body(d, c):
            rows_to(d, pack, buf, ss, rs).start()
            return c

        lax.fori_loop(1, sources, body, 0)
        wide = buf.shape[2]
        buf[pi, padded(me), :] = pack[padded(ei), pl.ds(pl.multiple_of(si * wide, LANES), wide)]
        forward(me, pi, buf, fss, frs).start()

    send_rows(px, bufx, x_send, x_recv, fx_send, fx_recv)

    loads[1].wait()
    scaled = (slot_weight * dot(pick, og[...])).astype(BF16)
    loads[2].wait()
    projected = dot(scaled, pj[...], NT).astype(BF16)
    lane = lax.broadcasted_iota(jnp.int32, (owners * PAD, LANES - rank_size), 1)
    extra = jnp.concatenate(
        [projected, jnp.where(lane == 0, slot_code, 0.0).astype(BF16)], axis=1
    )
    for s in range(subs):
        pz[:, s * zw : s * zw + dh] = scaled[:, s * dh : (s + 1) * dh]
        pz[:, s * zw + dh : (s + 1) * zw] = extra
    send_rows(pz, bufz, z_send, z_recv, fz_send, fz_recv)

    squeeze = pack_matrix(BLOCK, GROUP * PAD)

    def compact(half_at, buf, comp):
        def body(g, c):
            part = buf[half_at, pl.ds(pl.multiple_of(g * GROUP * PAD, GROUP * PAD), GROUP * PAD), :]
            at = pl.multiple_of(half_at * half + g * BLOCK, PAD)
            comp[pl.ds(at, BLOCK), :] = dot(squeeze, part).astype(BF16)
            return c

        lax.fori_loop(0, sources // GROUP, body, 0)

    def take_rows(buf, comp, ss, rs, fss, frs):
        def pass_on(d, c):
            j = lax.rem(me - d + sources, sources)
            pltpu.make_async_remote_copy(
                src_ref=buf.at[pi, padded(j)],
                dst_ref=buf.at[pi, padded(j)],
                send_sem=ss.at[j],
                recv_sem=rs.at[j],
                device_id={"expert": j // subs, "sub": j % subs},
                device_id_type=MESH,
            ).wait_recv()
            forward(j, pi, buf, fss, frs).start()
            return c

        lax.fori_loop(1, sources, pass_on, 0)
        compact(pi, buf, comp)

        def take_pass(j, c):
            forward(j, other, buf, fss, frs).wait_recv()
            return c

        lax.fori_loop(0, sources, take_pass, 0)
        compact(other, buf, comp)

    def gate_up(at, out, to):
        x = compx[pl.ds(at, BLOCK), :]
        out[pl.ds(to, BLOCK), 0:ff] = dot(x, gate[...]).astype(out.dtype)
        out[pl.ds(to, BLOCK), ff : 2 * ff] = dot(x, up[...]).astype(out.dtype)

    def grad(at, out, to):
        z = compz[pl.ds(at, BLOCK), 0:dh]
        out[pl.ds(to, BLOCK), :] = dot(z, down[...], NT).astype(out.dtype)

    def share_copy(d, src, buf, ss, rs, came):
        s = lax.rem(si + d, subs)
        at = s if came else si
        return pltpu.make_async_remote_copy(
            src_ref=buf.at[at] if came else src.at[pl.ds(pl.multiple_of(s * chunk, PAD), chunk)],
            dst_ref=buf.at[at],
            send_sem=ss.at[s],
            recv_sem=rs.at[at],
            device_id={"sub": s},
            device_id_type=MESH,
        )

    def exchange(work, src, own, buf, ss, rs):
        for d in range(1, subs):
            base = lax.rem(si + d, subs) * chunk

            def send_block(b, c):
                at = pl.multiple_of(base + b * BLOCK, PAD)
                work(at, src, at)
                return c

            lax.fori_loop(0, chunk // BLOCK, send_block, 0)
            share_copy(d, src, buf, ss, rs, False).start()

        def own_block(b, c):
            at = pl.multiple_of(si * chunk + b * BLOCK, PAD)
            work(at, own, pl.multiple_of(b * BLOCK, PAD))
            return c

        lax.fori_loop(0, chunk // BLOCK, own_block, 0)

    def summed(own, buf, to, k):
        v = own[pl.ds(to, BLOCK), k * ff : (k + 1) * ff]
        for d in range(1, subs):
            s = lax.rem(si + d, subs)
            v = v + buf[s, pl.ds(to, BLOCK), k * ff : (k + 1) * ff].astype(F32)
        return v

    take_rows(bufx, compx, x_send, x_recv, fx_send, fx_recv)
    loads[3].wait()
    loads[4].wait()
    exchange(gate_up, gu_send, gu_own, gu_buf, gu_ss, gu_rs)
    take_rows(bufz, compz, z_send, z_recv, fz_send, fz_recv)
    loads[5].wait()
    exchange(grad, hg_send, hg_own, hg_buf, hg_ss, hg_rs)

    hp_me = si * 2 + pi
    for d in range(1, subs):
        share_copy(d, gu_send, gu_buf, gu_ss, gu_rs, True).wait_recv()

    def hidden_block(b, c):
        to = pl.multiple_of(b * BLOCK, PAD)
        g, u = summed(gu_own, gu_buf, to, 0), summed(gu_own, gu_buf, to, 1)
        gu_own[pl.ds(to, BLOCK), 0:ff] = g
        gu_own[pl.ds(to, BLOCK), ff : 2 * ff] = u
        hidden = (g * (1.0 / (1.0 + jnp.exp(-g))) * u).astype(BF16)
        v = dot(hidden, ph[...], NT)
        hp_buf[hp_me, pl.ds(to, BLOCK), :] = jnp.concatenate(
            [v, jnp.zeros((BLOCK, LANES - rank_size), F32)], axis=1
        )
        return c

    lax.fori_loop(0, chunk // BLOCK, hidden_block, 0)

    def h_copy(d, came):
        q = lax.rem(hp_me + d, 2 * subs)
        at = q if came else hp_me
        return pltpu.make_async_remote_copy(
            src_ref=hp_buf.at[at],
            dst_ref=hp_buf.at[at],
            send_sem=h_ss.at[q],
            recv_sem=h_rs.at[at],
            device_id={"sub": q // 2, "pair": q % 2},
            device_id_type=MESH,
        )

    for d in range(1, 2 * subs):
        h_copy(d, False).start()
    for d in range(1, subs):
        share_copy(d, hg_send, hg_buf, hg_ss, hg_rs, True).wait_recv()

    def act_block(b, c):
        to = pl.multiple_of(b * BLOCK, PAD)
        g, u = gu_own[pl.ds(to, BLOCK), 0:ff], gu_own[pl.ds(to, BLOCK), ff : 2 * ff]
        h = summed(hg_own, hg_buf, to, 0)
        sig = 1.0 / (1.0 + jnp.exp(-g))
        at = pl.multiple_of(si * chunk + b * BLOCK, PAD)
        gbuf[pl.ds(at, BLOCK), 0:ff] = (h * u * sig * (1.0 + g * (1.0 - sig))).astype(BF16)
        gbuf[pl.ds(at, BLOCK), ff : 2 * ff] = (h * (g * sig)).astype(BF16)
        return c

    lax.fori_loop(0, chunk // BLOCK, act_block, 0)

    def g_copy(d, came):
        s = lax.rem(si + d, subs)
        at = s if came else si
        span = gbuf.at[pl.ds(pl.multiple_of(at * chunk, PAD), chunk)]
        return pltpu.make_async_remote_copy(
            src_ref=span,
            dst_ref=span,
            send_sem=g_ss.at[s],
            recv_sem=g_rs.at[at],
            device_id={"sub": s},
            device_id_type=MESH,
        )

    for d in range(1, subs):
        g_copy(d, False).start()

    rp, ret_send = compx, bufx.at[other]

    def swap(s):
        span = pl.ds(pl.multiple_of(s * chunk, PAD), chunk)
        return pltpu.make_async_remote_copy(
            src_ref=rp.at[span],
            dst_ref=rp_in.at[pl.ds(pl.multiple_of(s % (subs // 2) * chunk, PAD), chunk)],
            send_sem=p_ss.at[s],
            recv_sem=p_rs.at[s],
            device_id={"pair": other},
            device_id_type=MESH,
        )

    def back(j, came):
        at_e = j // subs if came else ei
        at_s = j % subs if came else si
        return pltpu.make_async_remote_copy(
            src_ref=ret_send.at[padded(j)],
            dst_ref=ret_buf.at[padded(at_e), pl.ds(pl.multiple_of(at_s * dh, LANES), dh)],
            send_sem=r_ss.at[j],
            recv_sem=r_rs.at[j if came else me],
            device_id={"expert": j // subs, "sub": j % subs},
            device_id_type=MESH,
        )

    per_chunk = chunk // CAP

    def route_chunk(s):
        def body(b, c):
            at = pl.multiple_of(s * chunk + b * BLOCK, PAD)
            v = dot(gbuf[pl.ds(at, BLOCK), 0:ff], gate[...], NT)
            v = v + dot(gbuf[pl.ds(at, BLOCK), ff : 2 * ff], up[...], NT)
            rp[pl.ds(at, BLOCK), :] = v.astype(BF16)
            return c

        lax.fori_loop(0, chunk // BLOCK, body, 0)
        first = s * per_chunk - pi * sources

        @pl.when(s * 2 // subs == other)
        def _():
            swap(s).start()

        @pl.when(s * 2 // subs == pi)
        def _():
            swap(s).wait_recv()

            def sum_block(b, c):
                at = pl.multiple_of(s * chunk + b * BLOCK, PAD)
                came = pl.multiple_of(s % (subs // 2) * chunk + b * BLOCK, PAD)
                v = rp[pl.ds(at, BLOCK), :].astype(F32) + rp_in[pl.ds(came, BLOCK), :].astype(F32)
                put = pl.multiple_of((first + b * GROUP) * PAD, GROUP * PAD)
                ret_send[pl.ds(put, GROUP * PAD), :] = dot(squeeze, v.astype(BF16), TN).astype(BF16)
                return c

            lax.fori_loop(0, chunk // BLOCK, sum_block, 0)

            def start_back(i, c):
                j = first + lax.rem(me + 1 + i, per_chunk)

                @pl.when(j != me)
                def _():
                    back(j, False).start()

                @pl.when(j == me)
                def _():
                    ret_buf[padded(ei), pl.ds(pl.multiple_of(si * dh, LANES), dh)] = ret_send[
                        padded(me), :
                    ]

                return c

            lax.fori_loop(0, per_chunk, start_back, 0)

    route_chunk(si)

    for d in range(1, 2 * subs):
        h_copy(d, True).wait_recv()
    share = rank_size // (2 * subs)
    spread_cols = gs.shape[0]
    row = lax.broadcasted_iota(jnp.int32, (LANES, spread_cols), 0)
    col = lax.broadcasted_iota(jnp.int32, (LANES, spread_cols), 1)
    repeat = jnp.where(row == hp_me * share + col % share, 1.0, 0.0).astype(BF16)
    want = (
        lax.broadcasted_iota(jnp.int32, (BLOCK, spread_cols), 1) // share + 1
    ).astype(F32)

    def example_block(b, acc):
        at = pl.multiple_of(b * BLOCK, PAD)
        ex = compz[pl.ds(at, BLOCK), dh:zw]
        code = ex[:, rank_size : rank_size + 1].astype(F32)
        spread = jnp.where(code == want, dot(ex, repeat), 0.0).astype(BF16)
        s = b // (chunk // BLOCK)
        to = pl.multiple_of((b % (chunk // BLOCK)) * BLOCK, PAD)
        hp = hp_buf[2 * s, pl.ds(to, BLOCK), :] + hp_buf[2 * s + 1, pl.ds(to, BLOCK), :]
        hi = hp.astype(BF16)
        rest = hp - hi.astype(F32)
        mid = rest.astype(BF16)
        low = (rest - mid.astype(F32)).astype(BF16)
        return acc + dot(spread, hi, TN) + dot(spread, mid, TN) + dot(spread, low, TN)

    gs[...] = lax.fori_loop(
        0, rows // BLOCK, example_block, jnp.zeros((spread_cols, LANES), F32)
    ).astype(BF16)
    piece = spread_cols // owners

    def e_copy(e, came):
        return pltpu.make_async_remote_copy(
            src_ref=gs.at[pl.ds(pl.multiple_of(e * piece, PAD), piece)],
            dst_ref=eg_buf.at[e if came else ei],
            send_sem=e_ss.at[e],
            recv_sem=e_rs.at[e if came else ei],
            device_id={"expert": e},
            device_id_type=MESH,
        )

    def start_e(d, c):
        e_copy(lax.rem(ei + d, owners), False).start()
        return c

    lax.fori_loop(1, owners, start_e, 0)
    eg_buf[ei] = gs[pl.ds(pl.multiple_of(ei * piece, PAD), piece), :]

    for d in range(1, subs):
        g_copy(d, True).wait_recv()
        route_chunk(lax.rem(si + d, subs))

    def take_e(d, c):
        e_copy(lax.rem(ei + d, owners), True).wait_recv()
        return c

    lax.fori_loop(1, owners, take_e, 0)
    eg = eg_buf[...].astype(F32)
    for x in range(4):
        eg_out[x] = eg[:, x * share : (x + 1) * share, 0:rank_size]

    def sent(d, c):
        j = lax.rem(me + d, sources)
        rows_to(d, px, bufx, x_send, x_recv).wait_send()
        rows_to(d, pz, bufz, z_send, z_recv).wait_send()
        back(j, False).wait_send()
        return c

    lax.fori_loop(1, sources, sent, 0)

    def sent_pass(j, c):
        forward(j, pi, bufx, fx_send, fx_recv).wait_send()
        forward(j, pi, bufz, fz_send, fz_recv).wait_send()
        return c

    lax.fori_loop(0, sources, sent_pass, 0)
    for d in range(1, subs):
        share_copy(d, gu_send, gu_buf, gu_ss, gu_rs, False).wait_send()
        share_copy(d, hg_send, hg_buf, hg_ss, hg_rs, False).wait_send()
        g_copy(d, False).wait_send()
    for d in range(1, 2 * subs):
        h_copy(d, False).wait_send()
    for i in range(subs // 2):
        swap(other * (subs // 2) + i).wait_send()

    def sent_e(d, c):
        e_copy(lax.rem(ei + d, owners), False).wait_send()
        return c

    lax.fori_loop(1, owners, sent_e, 0)

    def take_back(d, c):
        back(lax.rem(me + d, sources), True).wait_recv()
        return c

    lax.fori_loop(1, sources, take_back, 0)
    ret_out[...] = ret_buf[...]


def per_device(
    tokens, out_grad, routes, route_weight, example_id, gate_w, up_w, down_w, proj_grad, proj_hidden
):
    owners = lax.axis_size("expert")
    subs = lax.axis_size("sub")
    local_tokens, width = tokens.shape
    rank_size = proj_grad.shape[0]
    slots = owners * PAD
    dh = width // subs
    zw = dh + LANES
    ff = gate_w.shape[2]
    sources = owners * subs
    rows = sources * 2 * CAP
    chunk = rows // subs
    examples = 4 * owners
    share = rank_size // (2 * subs)
    piece = 4 * share
    vmem = pl.BlockSpec(memory_space=pltpu.VMEM)
    hbm = pl.BlockSpec(memory_space=pl.ANY)
    dma = pltpu.SemaphoreType.DMA

    def space(*shape, kind=BF16):
        return pltpu.VMEM(shape, kind)

    returned, pick_token, example_grads = pl.pallas_call(
        functools.partial(kernel, owners, subs, rank_size),
        out_shape=(
            jax.ShapeDtypeStruct((slots, width), BF16),
            jax.ShapeDtypeStruct((slots, local_tokens), BF16),
            jax.ShapeDtypeStruct((4, owners, share, rank_size), F32),
        ),
        in_specs=[vmem] * 3 + [hbm] * 6 + [vmem],
        out_specs=(vmem, vmem, vmem),
        scratch_shapes=[
            space(local_tokens, width),
            space(local_tokens, width),
            space(dh, ff),
            space(dh, ff),
            space(ff, dh),
            space(rank_size, width),
            space(slots, width),
            space(slots, subs * zw),
            space(2, sources * PAD, dh),
            space(2, sources * PAD, zw),
            space(rows, dh),
            space(rows, zw),
            space(rows, 2 * ff),
            space(chunk, 2 * ff, kind=F32),
            space(subs, chunk, 2 * ff),
            space(rows, ff),
            space(chunk, ff, kind=F32),
            space(subs, chunk, ff),
            space(rows, 2 * ff),
            space(2 * subs, chunk, LANES, kind=F32),
            space(rows // 2, dh),
            space(slots, width),
            space(examples * share, LANES),
            space(owners, piece, LANES),
            dma((6,)),
        ]
        + [dma((sources,))] * 8
        + [dma((subs,))] * 6
        + [dma((2 * subs,))] * 2
        + [dma((subs,))] * 2
        + [dma((sources,))] * 2
        + [dma((owners,))] * 2,
        compiler_params=pltpu.CompilerParams(
            collective_id=0, has_side_effects=True, vmem_limit_bytes=60 * 1024 * 1024
        ),
    )(
        routes.T, route_weight.T, example_id[None, :], tokens, out_grad,
        gate_w[0], up_w[0], down_w[0], proj_grad, proj_hidden,
    )
    input_grad = dot(pick_token, returned, TN).astype(BF16)
    return (input_grad, example_grads)


def solution(mesh):
    return jax.shard_map(
        per_device,
        mesh=mesh,
        in_specs=(
            P(("groups", "expert", "sub", "pair"), None),
            P(("groups", "expert", "sub", "pair"), None),
            P(("groups", "expert", "sub", "pair"), None),
            P(("groups", "expert", "sub", "pair"), None),
            P(("groups", "expert", "sub", "pair")),
            P("expert", "sub", "pair"),
            P("expert", "sub", "pair"),
            P("expert", "pair", "sub"),
            P(),
            P(None, "pair"),
        ),
        out_specs=(
            P(("groups", "expert", "sub", "pair"), None),
            P(("groups", "expert"), None, ("sub", "pair"), None),
        ),
        check_vma=False,
    )
```

time: 57.3 us -> 45.7 us (0.80)
  local copies, waits for them, and re-layouts: 6.86 us -> 0.66 us
  Pallas kernels: 46.4 us -> 42.1 us
  other arithmetic: 2.19 us -> 0 us
  matrix products: 0.79 us -> 2.12 us
    pallas_call x1, Pallas kernels: 46.4 us -> 42.1 us  [per_device(): pl.pallas_call(functools.partial(kernel, owners, subs, rank_size), out_sh...]
    unnamed x11 -> x3, local copies, waits for them, and re-layouts: 3.35 us -> 0.66 us
    convert_element_type x3 -> x0, other arithmetic: 2.05 us -> none  [the longest x1 0.7 us: per_device(): route_weight.astype(F32)[:, :, None]]
    concatenate x2 -> x0, local copies, waits for them, and re-layouts: 1.63 us -> none  [the longest x1 0.96 us: per_device(): payload = jnp.concatenate(parts, axis=1)]
    transpose x1 -> x0, local copies, waits for them, and re-layouts: 1.57 us -> none  [per_device(): return (input_grad, jnp.swapaxes(eg, 0, 1))]
    dot_general x4 -> x1, matrix products: 0.79 us -> 2.12 us  [dot(): return lax.dot_general(a, b, dims, preferred_element_type=F32)]
where the time goes in v2:
time: 45.7 us; the launch traced here: 45.5 us
  Pallas kernels  42.1 us (92%)
  matrix products  2.12 us (5%)
  local copies, waits for them, and re-layouts  0.66 us (1%)
  between operations  0.65 us (1%)
    pallas_call x1, Pallas kernels, per_device(): pl.pallas_call(functools.partial(kernel, owners, subs, rank_size), out_sh...  42.1 us
    dot_general x1, matrix products, dot(): return lax.dot_general(a, b, dims, preferred_element_type=F32)  2.12 us

profile of v2, /device:TPU:0, one launch (start us, length us, event | category | flops | bytes accessed | tf_op | source)
XLA Modules:
  0.0 45.5 jit_solution(17732144178272246821)
XLA Ops:
  0.6 42.1 %shard_map.113 = (bf16[64,2048]{1,0:T(8,128)(2,1)}, bf16[64,128]{1,0:T(8,128)(2,1)}, f32[4,4,16,64]{3,2,1,0:T(8,128)}) custom-call(s32[8,128]{1,0:T(8,128)} %bitcast.11, bf16[8,128]{1,0:T(8,128)(2,1)} %bitcast.12, s32[1,128]{1,0:T(1,128)} %bitcast.13, bf16[128,2048]{1,0:T(8,128)(2,1)} %tokens.1, bf16[128,2048]{1,0:T(8,128)(2,1)} %out_grad.1, ...), custom_call_target="tpu_custom_call" | custom-call | tf_op jit(solution)/shard_map/pallas_call | solution.py:505
  42.7 0.0 copy-start
  42.8 2.1 %convolution_convert_fusion = bf16[128,2048]{1,0:T(8,128)(2,1)} fusion(bf16[64,128]{1,0:T(8,128)(2,1)} %get-tuple-element.5, bf16[64,2048]{1,0:T(8,128)(2,1)} %get-tuple-element.6), kind=kOutput, calls=%fused_computation | convolution fusion | flops 33816576 | bytes 802816 | tf_op jit(solution)/shard_map/dot_general | solution.py:23
  44.9 0.0 copy-done
  44.9 0.7 %copy.13 = f32[4,4,16,64]{3,2,1,0:T(8,128)} copy(f32[4,4,16,64]{3,2,1,0:T(8,128)S(1)} %copy-done) | data formatting | bytes 131072
Async XLA Ops:
  42.7 2.1 %copy-start = (f32[4,4,16,64]{3,2,1,0:T(8,128)S(1)}, f32[4,4,16,64]{3,2,1,0:T(8,128)}, u32[]{:S(2)}) copy-start(f32[4,4,16,64]{3,2,1,0:T(8,128)} %get-tuple-element.11) | copy-start | bytes 196612

commit v3 on v2

--- a/solution.py
+++ b/solution.py
@@ -28,6 +28,38 @@
     k = lax.broadcasted_iota(jnp.int32, (rows, cols), 1)
     hit = (k // PAD == i // CAP) & (k % PAD == i % CAP)
     return jnp.where(hit, 1.0, 0.0).astype(BF16)
+
+
+def segments(tiles):
+    keep = -(-tiles * CAP // PAD)
+    found = {}
+    for f in range(CAP * (tiles - keep)):
+        k, i = divmod(f, PAD - CAP)
+        key = (k, keep + f // CAP)
+        lo, _, shift = found.get(key, (CAP + i, 0, CAP + i - f % CAP))
+        found[key] = (lo, CAP + i + 1, shift)
+    return keep, [(k, t) + v for (k, t), v in found.items()]
+
+
+def tile(k, n=1):
+    return slice(k * LANES, (k + n) * LANES)
+
+
+def mover(to_rows, to_step, from_rows, from_step, lo, hi, shift):
+    a = lax.broadcasted_iota(jnp.int32, (to_rows, from_rows), 0)
+    b = lax.broadcasted_iota(jnp.int32, (to_rows, from_rows), 1)
+    within = a % to_step
+    hit = (a // to_step == b // from_step) & (within - b % from_step == shift)
+    return jnp.where(hit & (within >= lo) & (within < hi), 1.0, 0.0).astype(BF16)
+
+
+def fold(value):
+    keep, segs = segments(value.shape[1] // LANES)
+    n = value.shape[0]
+    parts = [value[:, tile(k)].astype(F32) for k in range(keep)]
+    for k, t, lo, hi, shift in segs:
+        parts[k] = parts[k] + dot(mover(n, PAD, n, PAD, lo, hi, shift), value[:, tile(t)])
+    return jnp.concatenate([p.astype(BF16) for p in parts], axis=1)
 
 
 def kernel(
@@ -49,6 +81,7 @@
     chunk = rows // subs
     dh = compx.shape[1]
     zw = compz.shape[1]
+    wx, wz = bufx.shape[2], bufz.shape[2]
     ff = gate.shape[1]
 
     loads = [
@@ -98,7 +131,9 @@
     slot_code = jnp.concatenate(slot_codes, axis=0)
     pick_out[...] = pick
     loads[0].wait()
-    px[...] = dot(pick, tok[...]).astype(BF16)
+    picked = dot(pick, tok[...]).astype(BF16)
+    for s in range(subs):
+        px[:, s * wx : (s + 1) * wx] = fold(picked[:, s * dh : (s + 1) * dh])
     pl.semaphore_wait(barrier, sources - 1 + subs)
 
     def padded(j):
@@ -148,22 +183,36 @@
         [projected, jnp.where(lane == 0, slot_code, 0.0).astype(BF16)], axis=1
     )
     for s in range(subs):
-        pz[:, s * zw : s * zw + dh] = scaled[:, s * dh : (s + 1) * dh]
-        pz[:, s * zw + dh : (s + 1) * zw] = extra
+        pz[:, s * wz : (s + 1) * wz] = fold(
+            jnp.concatenate([scaled[:, s * dh : (s + 1) * dh], extra], axis=1)
+        )
     send_rows(pz, bufz, z_send, z_recv, fz_send, fz_recv)
 
     squeeze = pack_matrix(BLOCK, GROUP * PAD)
 
-    def compact(half_at, buf, comp):
+    def unfolders(tiles):
+        return [
+            (k, t, mover(BLOCK, CAP, GROUP * PAD, PAD, lo - shift, hi - shift, -shift))
+            for k, t, lo, hi, shift in segments(tiles)[1]
+        ]
+
+    def compact(half_at, buf, comp, moves):
+        keep = buf.shape[2] // LANES
+
         def body(g, c):
             part = buf[half_at, pl.ds(pl.multiple_of(g * GROUP * PAD, GROUP * PAD), GROUP * PAD), :]
             at = pl.multiple_of(half_at * half + g * BLOCK, PAD)
-            comp[pl.ds(at, BLOCK), :] = dot(squeeze, part).astype(BF16)
+            comp[pl.ds(at, BLOCK), tile(0, keep)] = dot(squeeze, part).astype(BF16)
+            for t in range(keep, comp.shape[1] // LANES):
+                v = sum(dot(m, part[:, tile(k)]) for k, to, m in moves if to == t)
+                comp[pl.ds(at, BLOCK), tile(t)] = v.astype(BF16)
             return c
 
         lax.fori_loop(0, sources // GROUP, body, 0)
 
     def take_rows(buf, comp, ss, rs, fss, frs):
+        moves = unfolders(comp.shape[1] // LANES)
+
         def pass_on(d, c):
             j = lax.rem(me - d + sources, sources)
             pltpu.make_async_remote_copy(
@@ -178,14 +227,14 @@
             return c
 
         lax.fori_loop(1, sources, pass_on, 0)
-        compact(pi, buf, comp)
+        compact(pi, buf, comp, moves)
 
         def take_pass(j, c):
             forward(j, other, buf, fss, frs).wait_recv()
             return c
 
         lax.fori_loop(0, sources, take_pass, 0)
-        compact(other, buf, comp)
+        compact(other, buf, comp, moves)
 
     def gate_up(at, out, to):
         x = compx[pl.ds(at, BLOCK), :]
@@ -323,7 +372,7 @@
         at_s = j % subs if came else si
         return pltpu.make_async_remote_copy(
             src_ref=ret_send.at[padded(j)],
-            dst_ref=ret_buf.at[padded(at_e), pl.ds(pl.multiple_of(at_s * dh, LANES), dh)],
+            dst_ref=ret_buf.at[padded(at_e), pl.ds(pl.multiple_of(at_s * wx, LANES), wx)],
             send_sem=r_ss.at[j],
             recv_sem=r_rs.at[j if came else me],
             device_id={"expert": j // subs, "sub": j % subs},
@@ -356,7 +405,14 @@
                 came = pl.multiple_of(s % (subs // 2) * chunk + b * BLOCK, PAD)
                 v = rp[pl.ds(at, BLOCK), :].astype(F32) + rp_in[pl.ds(came, BLOCK), :].astype(F32)
                 put = pl.multiple_of((first + b * GROUP) * PAD, GROUP * PAD)
-                ret_send[pl.ds(put, GROUP * PAD), :] = dot(squeeze, v.astype(BF16), TN).astype(BF16)
+                v = v.astype(BF16)
+                keep = wx // LANES
+                for k in range(keep):
+                    w = dot(squeeze, v[:, tile(k)], TN)
+                    for at_k, t, m in unfolders(dh // LANES):
+                        if at_k == k:
+                            w = w + dot(m, v[:, tile(t)], TN)
+                    ret_send[pl.ds(put, GROUP * PAD), tile(k)] = w.astype(BF16)
                 return c
 
             lax.fori_loop(0, chunk // BLOCK, sum_block, 0)
@@ -370,7 +426,7 @@
 
                 @pl.when(j == me)
                 def _():
-                    ret_buf[padded(ei), pl.ds(pl.multiple_of(si * dh, LANES), dh)] = ret_send[
+                    ret_buf[padded(ei), pl.ds(pl.multiple_of(si * wx, LANES), wx)] = ret_send[
                         padded(me), :
                     ]
 
@@ -475,7 +531,21 @@
         return c
 
     lax.fori_loop(1, sources, take_back, 0)
-    ret_out[...] = ret_buf[...]
+    keep, segs = segments(dh // LANES)
+    slots = ret_buf.shape[0]
+    moves = [
+        (k, t, mover(slots, PAD, slots, PAD, lo - shift, hi - shift, -shift))
+        for k, t, lo, hi, shift in segs
+    ]
+    for s in range(subs):
+        ret_out[:, s * dh : s * dh + wx] = ret_buf[:, s * wx : (s + 1) * wx]
+        for to in range(keep, dh // LANES):
+            v = sum(
+                dot(m, ret_buf[:, s * wx + k * LANES : s * wx + (k + 1) * LANES])
+                for k, t, m in moves
+                if t == to
+            )
+            ret_out[:, s * dh + to * LANES : s * dh + (to + 1) * LANES] = v.astype(BF16)
 
 
 def per_device(
@@ -488,6 +558,7 @@
     slots = owners * PAD
     dh = width // subs
     zw = dh + LANES
+    wx, wz = segments(dh // LANES)[0] * LANES, segments(zw // LANES)[0] * LANES
     ff = gate_w.shape[2]
     sources = owners * subs
     rows = sources * 2 * CAP
@@ -518,10 +589,10 @@
             space(dh, ff),
             space(ff, dh),
             space(rank_size, width),
-            space(slots, width),
-            space(slots, subs * zw),
-            space(2, sources * PAD, dh),
-            space(2, sources * PAD, zw),
+            space(slots, subs * wx),
+            space(slots, subs * wz),
+            space(2, sources * PAD, wx),
+            space(2, sources * PAD, wz),
             space(rows, dh),
             space(rows, zw),
             space(rows, 2 * ff),
@@ -533,7 +604,7 @@
             space(rows, 2 * ff),
             space(2 * subs, chunk, LANES, kind=F32),
             space(rows // 2, dh),
-            space(slots, width),
+            space(slots, subs * wx),
             space(examples * share, LANES),
             space(owners, piece, LANES),
             dma((6,)),

time: 45.7 us -> 41.1 us (0.90)
  Pallas kernels: 42.1 us -> 37.5 us
    pallas_call x1, Pallas kernels: 42.1 us -> 37.5 us  [per_device(): pl.pallas_call(functools.partial(kernel, owners, subs, rank_size), out_sh...]
where the time goes in v3:
time: 41.1 us; the launch traced here: 40.9 us
  Pallas kernels  37.5 us (91%)
  matrix products  2.12 us (5%)
  local copies, waits for them, and re-layouts  0.66 us (2%)
  between operations  0.65 us (2%)
    pallas_call x1, Pallas kernels, per_device(): pl.pallas_call(functools.partial(kernel, owners, subs, rank_size), out_sh...  37.5 us
    dot_general x1, matrix products, dot(): return lax.dot_general(a, b, dims, preferred_element_type=F32)  2.12 us

profile of v3, /device:TPU:0, one launch (start us, length us, event | category | flops | bytes accessed | tf_op | source)
XLA Modules:
  0.0 40.9 jit_solution(10326422424449616964)
XLA Ops:
  0.6 37.5 %shard_map.113 = (bf16[64,2048]{1,0:T(8,128)(2,1)}, bf16[64,128]{1,0:T(8,128)(2,1)}, f32[4,4,16,64]{3,2,1,0:T(8,128)}) custom-call(s32[8,128]{1,0:T(8,128)} %bitcast.11, bf16[8,128]{1,0:T(8,128)(2,1)} %bitcast.12, s32[1,128]{1,0:T(1,128)} %bitcast.13, bf16[128,2048]{1,0:T(8,128)(2,1)} %tokens.1, bf16[128,2048]{1,0:T(8,128)(2,1)} %out_grad.1, ...), custom_call_target="tpu_custom_call" | custom-call | tf_op jit(solution)/shard_map/pallas_call | solution.py:576
  38.2 0.0 copy-start
  38.2 2.1 %convolution_convert_fusion = bf16[128,2048]{1,0:T(8,128)(2,1)} fusion(bf16[64,128]{1,0:T(8,128)(2,1)} %get-tuple-element.5, bf16[64,2048]{1,0:T(8,128)(2,1)} %get-tuple-element.6), kind=kOutput, calls=%fused_computation | convolution fusion | flops 33816576 | bytes 802816 | tf_op jit(solution)/shard_map/dot_general | solution.py:23
  40.3 0.0 copy-done
  40.3 0.7 %copy.13 = f32[4,4,16,64]{3,2,1,0:T(8,128)} copy(f32[4,4,16,64]{3,2,1,0:T(8,128)S(1)} %copy-done) | data formatting | bytes 131072
Async XLA Ops:
  38.2 2.1 %copy-start = (f32[4,4,16,64]{3,2,1,0:T(8,128)S(1)}, f32[4,4,16,64]{3,2,1,0:T(8,128)}, u32[]{:S(2)}) copy-start(f32[4,4,16,64]{3,2,1,0:T(8,128)} %get-tuple-element.11) | copy-start | bytes 196612

commit v4 on v3

--- a/solution.py
+++ b/solution.py
@@ -90,8 +90,7 @@
             [(tokens, tok), (out_grad, og), (proj, pj), (gate_in, gate), (up_in, up), (down_in, down)]
         )
     ]
-    for load in loads:
-        load.start()
+    loads[0].start()
 
     barrier = pltpu.get_barrier_semaphore()
 
@@ -131,6 +130,8 @@
     slot_code = jnp.concatenate(slot_codes, axis=0)
     pick_out[...] = pick
     loads[0].wait()
+    for load in loads[1:]:
+        load.start()
     picked = dot(pick, tok[...]).astype(BF16)
     for s in range(subs):
         px[:, s * wx : (s + 1) * wx] = fold(picked[:, s * dh : (s + 1) * dh])

time: 41.1 us -> 41.2 us (level)
  no operation moved by 1% of the time
where the time goes in v4:
time: 41.2 us; the launch traced here: 40.9 us
  Pallas kernels  37.5 us (91%)
  matrix products  2.12 us (5%)
  local copies, waits for them, and re-layouts  0.66 us (2%)
  between operations  0.65 us (2%)
    pallas_call x1, Pallas kernels, per_device(): pl.pallas_call(functools.partial(kernel, owners, subs, rank_size), out_sh...  37.5 us
    dot_general x1, matrix products, dot(): return lax.dot_general(a, b, dims, preferred_element_type=F32)  2.12 us

profile of v4, /device:TPU:0, one launch (start us, length us, event | category | flops | bytes accessed | tf_op | source)
XLA Modules:
  0.0 40.9 jit_solution(14737712474982044070)
XLA Ops:
  0.6 37.5 %shard_map.113 = (bf16[64,2048]{1,0:T(8,128)(2,1)}, bf16[64,128]{1,0:T(8,128)(2,1)}, f32[4,4,16,64]{3,2,1,0:T(8,128)}) custom-call(s32[8,128]{1,0:T(8,128)} %bitcast.11, bf16[8,128]{1,0:T(8,128)(2,1)} %bitcast.12, s32[1,128]{1,0:T(1,128)} %bitcast.13, bf16[128,2048]{1,0:T(8,128)(2,1)} %tokens.1, bf16[128,2048]{1,0:T(8,128)(2,1)} %out_grad.1, ...), custom_call_target="tpu_custom_call" | custom-call | tf_op jit(solution)/shard_map/pallas_call | solution.py:577
  38.2 0.0 copy-start
  38.2 2.1 %convolution_convert_fusion = bf16[128,2048]{1,0:T(8,128)(2,1)} fusion(bf16[64,128]{1,0:T(8,128)(2,1)} %get-tuple-element.5, bf16[64,2048]{1,0:T(8,128)(2,1)} %get-tuple-element.6), kind=kOutput, calls=%fused_computation | convolution fusion | flops 33816576 | bytes 802816 | tf_op jit(solution)/shard_map/dot_general | solution.py:23
  40.3 0.0 copy-done
  40.3 0.7 %copy.13 = f32[4,4,16,64]{3,2,1,0:T(8,128)} copy(f32[4,4,16,64]{3,2,1,0:T(8,128)S(1)} %copy-done) | data formatting | bytes 131072
Async XLA Ops:
  38.2 2.1 %copy-start = (f32[4,4,16,64]{3,2,1,0:T(8,128)S(1)}, f32[4,4,16,64]{3,2,1,0:T(8,128)}, u32[]{:S(2)}) copy-start(f32[4,4,16,64]{3,2,1,0:T(8,128)} %get-tuple-element.11) | copy-start | bytes 196612

commit v5 on v3

--- a/solution.py
+++ b/solution.py
@@ -546,6 +546,10 @@
                 if t == to
             )
             ret_out[:, s * dh + to * LANES : s * dh + (to + 1) * LANES] = v.astype(BF16)
+
+
+def spread_rows(pick, rows, out):
+    out[...] = dot(pick[...], rows[...], TN).astype(BF16)
 
 
 def per_device(
@@ -622,7 +626,12 @@
         routes.T, route_weight.T, example_id[None, :], tokens, out_grad,
         gate_w[0], up_w[0], down_w[0], proj_grad, proj_hidden,
     )
-    input_grad = dot(pick_token, returned, TN).astype(BF16)
+    input_grad = pl.pallas_call(
+        spread_rows,
+        out_shape=jax.ShapeDtypeStruct((local_tokens, width), BF16),
+        in_specs=[vmem] * 2,
+        out_specs=vmem,
+    )(pick_token, returned)
     return (input_grad, example_grads)
 
 

time: 41.1 us -> 41.1 us (level)
  matrix products: 2.12 us -> 0 us
  Pallas kernels: 37.5 us -> 39.6 us
    pallas_call x0 -> x1, Pallas kernels: none -> 2.12 us  [per_device(): pl.pallas_call(spread_rows, out_shape=jax.ShapeDtypeStruct((local_tokens,...]
    dot_general x1 -> x0, matrix products: 2.12 us -> none  [dot(): return lax.dot_general(a, b, dims, preferred_element_type=F32)]
where the time goes in v5:
time: 41.1 us; the launch traced here: 40.9 us
  Pallas kernels  39.6 us (96%)
  local copies, waits for them, and re-layouts  0.66 us (2%)
  between operations  0.65 us (2%)
    pallas_call x1, Pallas kernels, per_device(): pl.pallas_call(functools.partial(kernel, owners, subs, rank_size), out_sh...  37.5 us
    pallas_call x1, Pallas kernels, per_device(): pl.pallas_call(spread_rows, out_shape=jax.ShapeDtypeStruct((local_tokens,...  2.12 us

profile of v5, /device:TPU:0, one launch (start us, length us, event | category | flops | bytes accessed | tf_op | source)
XLA Modules:
  0.0 40.9 jit_solution(9387826960505311539)
XLA Ops:
  0.6 37.5 %shard_map.113 = (bf16[64,2048]{1,0:T(8,128)(2,1)}, bf16[64,128]{1,0:T(8,128)(2,1)}, f32[4,4,16,64]{3,2,1,0:T(8,128)}) custom-call(s32[8,128]{1,0:T(8,128)} %bitcast.9, bf16[8,128]{1,0:T(8,128)(2,1)} %bitcast.10, s32[1,128]{1,0:T(1,128)} %bitcast.11, bf16[128,2048]{1,0:T(8,128)(2,1)} %tokens.1, bf16[128,2048]{1,0:T(8,128)(2,1)} %out_grad.1, ...), custom_call_target="tpu_custom_call" | custom-call | tf_op jit(solution)/shard_map/pallas_call | solution.py:580
  38.2 0.0 copy-start
  38.2 2.1 %shard_map.114 = bf16[128,2048]{1,0:T(8,128)(2,1)} custom-call(bf16[64,128]{1,0:T(8,128)(2,1)} %get-tuple-element.5.pick, bf16[64,2048]{1,0:T(8,128)(2,1)} %get-tuple-element.6.rows), custom_call_target="tpu_custom_call" | custom-call | tf_op jit(solution)/shard_map/pallas_call | solution.py:629
  40.3 0.0 copy-done
  40.3 0.7 %copy.13 = f32[4,4,16,64]{3,2,1,0:T(8,128)} copy(f32[4,4,16,64]{3,2,1,0:T(8,128)S(1)} %copy-done) | data formatting | bytes 131072
Async XLA Ops:
  38.2 2.1 %copy-start = (f32[4,4,16,64]{3,2,1,0:T(8,128)S(1)}, f32[4,4,16,64]{3,2,1,0:T(8,128)}, u32[]{:S(2)}) copy-start(f32[4,4,16,64]{3,2,1,0:T(8,128)} %get-tuple-element.11) | copy-start | bytes 196612
